TPU v7x, 128 devices: a whole 4x4x4 slice. The times are simulated.
128 devices in a mesh: wide: 32 (over x_hi, y, z), narrow: 4 (over x_lo, core).
Axes of the slice: x: 4 (x_hi: 2, x_lo: 2; x = x_hi * 2 + x_lo), y: 4, z: 4, core: 2. Of those that a mesh axis runs over, the one named last changes fastest.
Arguments:
- tokens: bfloat16 [128, 257, 1664], P(('wide', 'narrow')), may hold values from -6 to 6
- cotangent: bfloat16 [128, 257, 1664], P(('wide', 'narrow')), may hold values from -24 to 24
- ln_gain: float32 [1664], replicated, may hold values from 0.1 to 1.9
- w_qkv: bfloat16 [4992, 1664], replicated, may hold values from -6 to 6, as said below
- w_out: bfloat16 [1664, 1664], replicated, may hold values from -0.15625 to 0.15625
Outputs:
- grad_input: bfloat16 [128, 257, 1664], P(('wide', 'narrow'))
- grad_qkv: float32 [4992, 1664], P('wide')
- grad_out: float32 [1664, 1664], P('wide')
- grad_gain: float32 [1664], replicated
Inputs may be any that keep to these rules, and one draw needn't show every extreme that they name: `w_qkv`: rows [0, 1664) project to queries, [1664, 3328) to keys, the rest to values.
All inputs are finite; a program needn't handle non-finite values.
Results may differ from a plain program's by a relative error of at most 0.03.
Values may be sent and summed in bfloat16 or wider, within the bound.
A program may use at most 128 MiB of HBM per device.

v0:
```python
import functools

import jax
import jax.numpy as jnp
from jax import lax
from jax.experimental import pallas as pl
from jax.experimental.pallas import tpu as pltpu
from jax.sharding import PartitionSpec as P

HEADS = 16


ln_epsilon = 1e-06


LANES = 128
WINDOW = 256


def dot(a, b, over=((1,), (0,))):
    return lax.dot_general(a, b, (over, ((), ())), preferred_element_type=jnp.float32)


def low(a):
    return a.astype(jnp.bfloat16)


def normalise(x_ref):
    x = x_ref[...].astype(jnp.float32)
    centered = x - jnp.mean(x, axis=-1, keepdims=True)
    inv_sigma = lax.rsqrt(jnp.mean(centered * centered, axis=-1, keepdims=True) + ln_epsilon)
    return centered * inv_sigma, inv_sigma


def front_kernel(scale, x_ref, cot_ref, gain_ref, w_ref, wo_ref,
                 lno_ref, ao_ref, gt_ref, gx_ref, gg_ref, wpad, gln):
    h = pl.program_id(0)
    dim = w_ref.shape[2]

    @pl.when(h == 0)
    def _():
        normed, _ = normalise(x_ref)
        lno_ref[...] = low(normed * gain_ref[...])
        wpad[...] = jnp.zeros_like(wpad)
        gln[...] = jnp.zeros_like(gln)

    for s in range(3):
        wpad[s * LANES : s * LANES + dim, :] = w_ref[s, 0]
    qkv = low(dot(lno_ref[...], wpad[...], ((1,), (1,))))
    q, k, v = (qkv[:, s * LANES : (s + 1) * LANES] for s in range(3))
    scores = dot(q, k, ((1,), (1,))) * scale
    expo = jnp.exp(scores - jnp.max(scores, axis=-1, keepdims=True))
    prob = expo / jnp.sum(expo, axis=-1, keepdims=True)
    prob_low = low(prob)

    start = jnp.minimum(lax.div(h * dim, LANES) * LANES, wo_ref.shape[1] - WINDOW)
    start = pl.multiple_of(start, LANES)
    offset = h * dim - start
    lane = lax.broadcasted_iota(jnp.int32, (1, WINDOW), 1)
    attn = dot(prob_low, v)
    attn = jnp.concatenate([attn, jnp.zeros_like(attn)], axis=1)
    attn = pltpu.roll(attn, offset, 1)
    window = ao_ref[:, pl.ds(start, WINDOW)].astype(jnp.float32)
    inside = jnp.logical_and(lane >= offset, lane < offset + dim)
    ao_ref[:, pl.ds(start, WINDOW)] = low(jnp.where(inside, attn, window))

    grad = dot(cot_ref[...], wo_ref[:, pl.ds(start, WINDOW)])
    grad = pltpu.roll(grad, lax.rem(WINDOW - offset, WINDOW), 1)[:, :LANES]
    grad = low(jnp.where(lane[:, :LANES] < dim, grad, 0.0))
    grad_prob = dot(grad, v, ((1,), (1,)))
    inner = jnp.sum(grad_prob * prob, axis=-1, keepdims=True)
    grad_score = low(prob * (grad_prob - inner) * scale)

    gq = low(dot(grad_score, k)).astype(jnp.float32)
    gkt = low(dot(q, grad_score, ((0,), (0,)))).astype(jnp.float32)
    gvt = low(dot(grad, prob_low, ((0,), (0,)))).astype(jnp.float32)
    gt_ref[0, 0] = low(gq.T[:dim])
    gt_ref[1, 0] = low(gkt[:dim])
    gt_ref[2, 0] = low(gvt[:dim])
    gcat = low(jnp.concatenate([gq, gkt.T, gvt.T], axis=1))
    gln[...] += dot(gcat, wpad[...])

    @pl.when(h == pl.num_programs(0) - 1)
    def _():
        normed, inv_sigma = normalise(x_ref)
        grad_ln = gln[...]
        total = jnp.sum(grad_ln * normed, axis=0, keepdims=True)
        row = lax.broadcasted_iota(jnp.int32, gg_ref.shape, 0)
        gg_ref[...] = jnp.where(row == 0, total, 0.0)
        g = grad_ln * gain_ref[...]
        grad_x = inv_sigma * (
            g - jnp.mean(g, axis=-1, keepdims=True) - normed * jnp.mean(g * normed, axis=-1, keepdims=True)
        )
        gx_ref[...] = low(cot_ref[...].astype(jnp.float32) + grad_x)


def front_call(x, cot, gain, w_qkv, w_out):
    tok, width = x.shape
    dim = width // HEADS
    whole = lambda a: pl.BlockSpec(a.shape, lambda h: (0,) * len(a.shape))
    w = w_qkv.reshape(3, HEADS, dim, width)
    gain = gain.reshape(1, width)
    outs = (
        jax.ShapeDtypeStruct((tok, width), jnp.bfloat16),
        jax.ShapeDtypeStruct((tok, width), jnp.bfloat16),
        jax.ShapeDtypeStruct((3, HEADS, dim, tok), jnp.bfloat16),
        jax.ShapeDtypeStruct((tok, width), jnp.bfloat16),
        jax.ShapeDtypeStruct((8, width), jnp.float32),
    )
    return pl.pallas_call(
        functools.partial(front_kernel, dim**-0.5),
        grid=(HEADS,),
        out_shape=outs,
        in_specs=[whole(x), whole(cot), whole(gain), pl.BlockSpec((3, 1, dim, width), lambda h: (0, h, 0, 0)), whole(w_out)],
        out_specs=[whole(outs[0]), whole(outs[1]), pl.BlockSpec((3, 1, dim, tok), lambda h: (0, h, 0, 0)), whole(outs[3]), whole(outs[4])],
        scratch_shapes=[pltpu.VMEM((3 * LANES, width), jnp.bfloat16), pltpu.VMEM((tok, width), jnp.float32)],
        compiler_params=pltpu.CompilerParams(vmem_limit_bytes=56 * 2**20, dimension_semantics=("arbitrary",)),
        cost_estimate=pl.CostEstimate(flops=12 * 10**9, bytes_accessed=26 * 2**20, transcendentals=HEADS * tok * tok),
    )(x, cot, gain, w, w_out)


BLOCKS = 32
ROWS = 208
Q_ROWS = 156
PARTS = ((0, 80), (80, 64), (144, 64))
CUTS = (48, 32, 32)


def rem(a, b):
    return lax.rem(a, jnp.int32(b))


def div(a, b):
    return lax.div(a, jnp.int32(b))


def reduce_kernel(factor, gt, ct, lno, ao, gain_in, out, gain_out,
                  S, R0, T0, A1, A2, A3, B1, B2, B3, E1, E2, E3, C1, C2, C3, T1, F, G,
                  s0, r0, s1, r1, s2, r2, s3, r3, s4, r4, sg, rg):
    cols = lno.shape[1]
    wide, narrow = lax.axis_index("wide"), lax.axis_index("narrow")
    xh, y, z = div(wide, 16), rem(div(wide, 4), 4), rem(wide, 4)
    xl, c = div(narrow, 2), rem(narrow, 2)
    x = 2 * xh + xl

    def device(x_, y_, z_, c_):
        return (div(x_, 2) * 16 + y_ * 4 + z_, rem(x_, 2) * 2 + c_)

    def shift(dim, by):
        at = [x, y, z]
        at[dim] = rem(at[dim] + by, 4)
        return device(*at, c)

    place = (x, y, z)
    mate = device(x, y, z, 1 - c)
    peers = [mate] + [shift(d, by) for d in range(3) for by in (1, 2, 3)]
    barrier = pltpu.get_barrier_semaphore()
    for peer in peers:
        pl.semaphore_signal(barrier, inc=1, device_id=peer, device_id_type=pl.DeviceIdType.MESH)
    pl.semaphore_wait(barrier, len(peers))

    sent = []

    def send(src, dst, ssem, rsem, to):
        copy = pltpu.make_async_remote_copy(src_ref=src, dst_ref=dst, send_sem=ssem, recv_sem=rsem,
                                            device_id=to, device_id_type=pl.DeviceIdType.MESH)
        copy.start()
        return copy

    def gain_stage(k, n, m, to):
        G[k, m] = gain_out[...] if k else gain_in[...]
        copies = [send(G.at[k, m], G.at[k, m], sg.at[k, r], rg.at[k, r], to(r + 1)) for r in range(n - 1)]
        for copy in copies:
            copy.wait()
        total = G[k, 0]
        for other in range(1, n):
            total = total + G[k, other]
        gain_out[...] = total

    def fill(dst, b, left):
        first, last = left[0:160], left[144:208]
        row = lax.broadcasted_iota(jnp.int32, (16, 1), 0)
        for lo, hi in ((0, 512), (512, 1024), (1024, cols)):
            p = jnp.dot(first, lno[:, lo:hi], preferred_element_type=jnp.float32) * factor
            q = jnp.dot(last, ao[:, lo:hi], preferred_element_type=jnp.float32) * factor
            dst[b, 0:144, lo:hi] = p[0:144].astype(jnp.bfloat16)
            dst[b, 144:160, lo:hi] = jnp.where(row < Q_ROWS - 144, p[144:160], q[0:16]).astype(jnp.bfloat16)
            dst[b, 160:208, lo:hi] = q[16:64].astype(jnp.bfloat16)

    def rows_of_pair(b):
        g = jnp.concatenate([gt[3 * b + i].astype(jnp.float32) for i in range(3)], axis=0)
        d = ct[b].astype(jnp.float32)
        out_rows = ROWS - Q_ROWS
        return tuple(
            jnp.concatenate([g[i * Q_ROWS : (i + 1) * Q_ROWS], d[i * out_rows : (i + 1) * out_rows]], axis=0)
            for i in range(2)
        )

    def core_copy(b):
        return pltpu.make_async_remote_copy(src_ref=T0.at[b], dst_ref=R0.at[b], send_sem=s0.at[b], recv_sem=r0.at[b],
                                            device_id=mate, device_id_type=pl.DeviceIdType.MESH)

    @pl.loop(0, 16)
    def _(b):
        even, odd = rows_of_pair(b)
        mine_odd = rem(c + div(b, 8) + rem(div(b, 2), 4), 2) == 1
        fill(T0, b, jnp.where(mine_odd, even, odd).astype(jnp.bfloat16))
        core_copy(b).start()
        fill(S, b, jnp.where(mine_odd, odd, even).astype(jnp.bfloat16))

    def accumulate(dst, *more):
        total = dst[...].astype(jnp.float32)
        for term in more:
            total = total + term[...].astype(jnp.float32)
        dst[...] = total.astype(jnp.bfloat16)

    @pl.loop(0, 16)
    def _(b):
        core_copy(b).wait()
        accumulate(S.at[b], R0.at[b])

    def y_block(t, i):
        return (i // 2) * 8 + t * 2 + i % 2

    def z_block(t, i):
        return (i // 2) * 8 + (2 * (i % 2) + rem(c + t + i // 2, 2)) * 2 + div(t, 2)

    def x_block(t, i):
        return div(t, 2) * 8 + i * 2 + rem(t, 2)

    def yz_block(t):
        return rem(c + y + t, 2) * 8 + y * 2 + div(t, 2)

    def zx_block(t):
        return div(t, 2) * 8 + (2 * rem(t, 2) + rem(c + z + div(t, 2), 2)) * 2 + div(z, 2)

    def xy_block(t):
        return div(x, 2) * 8 + t * 2 + rem(x, 2)

    orders = ((1, 2, 0), (2, 0, 1), (0, 1, 2))
    firsts = (y_block, z_block, x_block)
    seconds = (yz_block, zx_block, xy_block)
    halves1, wholes1 = (A1, B1, E1), (A2, B2, E2)
    later = (A3, B3, E3)

    def part(p, b):
        return S.at[b, pl.ds(*PARTS[p]), :]

    for p in range(3):
        d = orders[p][0]
        m = place[d]
        t = rem(m + 2, 4)
        for i in range(2):
            sent.append(send(part(p, firsts[p](t, i)), halves1[p].at[0, i], s1.at[p, 0, i], r1.at[p, 0, i], shift(d, 1)))
            sent.append(send(part(p, firsts[p](t, 2 + i)), halves1[p].at[1, i], s1.at[p, 1, i], r1.at[p, 1, i], shift(d, 3)))
    step1 = list(sent)

    def pass_on(p, side, i):
        d = orders[p][0]
        t = rem(place[d] + (1 if side == 0 else 3), 4)
        copy = send(part(p, firsts[p](t, i)), wholes1[p].at[side, i], s2.at[p, side, i], r2.at[p, side, i],
                    shift(d, 1 if side == 0 else 3))
        sent.append(copy)
        return copy

    step2 = {}
    for p in range(3):
        for i in range(2):
            step2[p, 0, 2 + i] = pass_on(p, 0, 2 + i)
            step2[p, 1, i] = pass_on(p, 1, i)
    n = 0
    for p in range(3):
        d = orders[p][0]
        for i in range(2):
            for side in range(2):
                step1[n].wait_recv()
                n += 1
                t = rem(place[d] + (1 if side == 0 else 3), 4)
                index = i if side == 0 else 2 + i
                accumulate(part(p, firsts[p](t, index)), halves1[p].at[side, i])
                step2[p, side, index] = pass_on(p, side, index)

    gain_stage(0, 2, c, lambda r: mate)
    gain_stage(1, 4, x, lambda r: shift(0, r))
    gain_stage(2, 4, y, lambda r: shift(1, r))
    gain_stage(3, 4, z, lambda r: shift(2, r))

    step3 = {}
    for p in range(3):
        d, e = orders[p][0], orders[p][1]
        cut, size = CUTS[p], PARTS[p][1]
        low, high = pl.ds(0, cut), pl.ds(cut, size - cut)
        for i in range(4):
            step2[p, 0, i].wait_recv()
            step2[p, 1, i].wait_recv()
            accumulate(part(p, firsts[p](place[d], i)), wholes1[p].at[0, i], wholes1[p].at[1, i])
        m = place[e]
        opposite = part(p, seconds[p](rem(m + 2, 4)))
        right, left = part(p, seconds[p](rem(m + 1, 4))), part(p, seconds[p](rem(m + 3, 4)))
        inbox = later[p]
        for k, (what, rows, slot, by) in enumerate((
                (opposite, low, 0, 1), (opposite, high, 0, 3), (right, high, 1, 1), (left, low, 2, 3))):
            step3[p, k] = send(what.at[rows], inbox.at[slot, rows], s3.at[p, k], r3.at[p, k], shift(e, by))
            sent.append(step3[p, k])
    for p in range(3):
        e = orders[p][1]
        cut, size = CUTS[p], PARTS[p][1]
        low, high = pl.ds(0, cut), pl.ds(cut, size - cut)
        m = place[e]
        right, left = part(p, seconds[p](rem(m + 1, 4))), part(p, seconds[p](rem(m + 3, 4)))
        inbox = later[p]
        for k, (what, rows, slot, by) in enumerate(((right, low, 1, 1), (left, high, 2, 3))):
            step3[p, k].wait_recv()
            accumulate(what.at[rows], inbox.at[0, rows])
            step3[p, 4 + k] = send(what.at[rows], inbox.at[slot, rows], s3.at[p, 4 + k], r3.at[p, 4 + k], shift(e, by))
            sent.append(step3[p, 4 + k])
    mine = []
    for p in range(3):
        e = orders[p][1]
        for k in range(2, 6):
            step3[p, k].wait_recv()
        own = part(p, seconds[p](place[e]))
        accumulate(own, later[p].at[1], later[p].at[2])
        mine.append(own)

    chosen = c == rem(xh + y + z, 2)
    partner = device(2 * xh + 1 - xl, y, z, c)

    def final(p):
        return F.at[pl.ds(*PARTS[p]), :]

    def third(copy_of, slot, p, to):
        return pltpu.make_async_remote_copy(src_ref=copy_of, dst_ref=slot, send_sem=s4.at[p], recv_sem=r4.at[p],
                                            device_id=to, device_id_type=pl.DeviceIdType.MESH)

    outward = device(rem(x + 3 + 2 * xl, 4), y, z, c)
    to_pair = third(mine[0], C1.at[0], 0, outward)
    swap = third(T1, C1.at[1], 1, partner)

    y_to = 2 * xl + rem(c + z + xh, 2)
    z_to = 2 * xl + rem(c + y + xh, 2)
    reach = ((1, 2, C2, y_to, y, lambda: device(x, y_to, z, c)), (2, 5, C3, z_to, z, lambda: device(x, y, z_to, c)))

    @pl.when(jnp.logical_not(chosen))
    def _():
        to_pair.start()

    for p, base, slots, to, at, where in reach:
        for r in range(3):
            @pl.when(rem(at - to + 4, 4) == r + 1)
            def _():
                third(mine[p], slots.at[r], base + r, where()).start()

    @pl.when(chosen)
    def _():
        to_pair.wait_recv()
        T1[...] = (mine[0][...].astype(jnp.float32) + C1[0].astype(jnp.float32)).astype(jnp.bfloat16)
        swap.start()

    share = {1: third(final(1), final(1), 8, partner), 2: third(final(2), final(2), 9, partner)}
    for p, base, slots, to, at, where in reach:
        @pl.when(at == to)
        def _():
            for r in range(3):
                third(mine[p], slots.at[r], base + r, mate).wait_recv()
            total = mine[p][...].astype(jnp.float32)
            for r in range(3):
                total = total + slots[r].astype(jnp.float32)
            F[pl.ds(*PARTS[p]), :] = total.astype(jnp.bfloat16)
            share[p].start()

    give = third(F, F, 10, mate)

    @pl.when(chosen)
    def _():
        swap.wait_recv()
        F[pl.ds(*PARTS[0]), :] = (T1[...].astype(jnp.float32) + C1[1].astype(jnp.float32)).astype(jnp.bfloat16)

    for p, base, slots, to, at, where in reach:
        @pl.when(jnp.logical_and(chosen, at != to))
        def _():
            share[p].wait_recv()

    @pl.when(chosen)
    def _():
        give.start()

    @pl.when(jnp.logical_not(chosen))
    def _():
        give.wait_recv()

    out[...] = F[...].astype(jnp.float32)

    for copy in sent:
        copy.wait_send()

    @pl.when(chosen)
    def _():
        swap.wait_send()
        give.wait_send()

    @pl.when(jnp.logical_not(chosen))
    def _():
        to_pair.wait_send()

    for p, base, slots, to, at, where in reach:
        @pl.when(at == to)
        def _():
            share[p].wait_send()

        for r in range(3):
            @pl.when(rem(at - to + 4, 4) == r + 1)
            def _():
                third(mine[p], slots.at[r], base + r, where()).wait_send()


def reduce_call(gt, ct, lno, ao, gain, factor):
    cols = lno.shape[1]
    bf = lambda *shape: pltpu.VMEM(shape, jnp.bfloat16)
    sizes = [size for _, size in PARTS]
    dma = pltpu.SemaphoreType.DMA
    vm = pl.BlockSpec(memory_space=pltpu.VMEM)
    return pl.pallas_call(
        functools.partial(reduce_kernel, factor),
        out_shape=(jax.ShapeDtypeStruct((ROWS, cols), jnp.float32), jax.ShapeDtypeStruct((8, cols), jnp.float32)),
        in_specs=[vm] * 5,
        out_specs=[vm] * 2,
        scratch_shapes=(
            [bf(16, ROWS, cols)] * 3
            + [x for s in sizes for x in (bf(2, 2, s, cols), bf(2, 4, s, cols), bf(3, s, cols))]
            + [bf(2, sizes[0], cols), bf(3, sizes[1], cols), bf(3, sizes[2], cols), bf(sizes[0], cols), bf(ROWS, cols),
               pltpu.VMEM((4, 4, 8, cols), jnp.float32)]
            + [dma((16,))] * 2 + [dma((3, 2, 2))] * 2 + [dma((3, 2, 4))] * 2 + [dma((3, 6))] * 2 + [dma((11,))] * 2
            + [dma((4, 3))] * 2
        ),
        compiler_params=pltpu.CompilerParams(collective_id=0, has_side_effects=True, vmem_limit_bytes=62 * 2**20),
        cost_estimate=pl.CostEstimate(flops=2 * BLOCKS * ROWS * lno.shape[0] * cols, bytes_accessed=2**24, transcendentals=0),
    )(gt, ct, lno, ao, gain)


def local(tokens, cotangent, ln_gain, w_qkv, w_out):
    images = tokens.shape[0] * lax.axis_size("wide") * lax.axis_size("narrow")
    factor = 1.0 / images
    x, cot = tokens[0], cotangent[0]
    ln_out, attn_out, grad_t, grad_input, gain = front_call(x, cot, ln_gain, w_qkv, w_out)
    cot_t = cot.T.reshape(BLOCKS // 2, -1, cot.shape[0])
    grad_t = grad_t.reshape(BLOCKS * 3 // 2, -1, cot.shape[0])
    total, gain = reduce_call(grad_t, cot_t, ln_out, attn_out, gain, factor)
    return (grad_input[None], total[:Q_ROWS], total[Q_ROWS:], gain[0] * factor)


def solution(mesh):
    return jax.shard_map(
        local,
        mesh=mesh,
        in_specs=(
            P(("wide", "narrow"), None, None),
            P(("wide", "narrow"), None, None),
            P(),
            P(),
            P(),
        ),
        out_specs=(P(("wide", "narrow"), None, None), P("wide", None), P("wide", None), P()),
        check_vma=False,
    )
```

profile of v0, /device:TPU:1, one launch (start us, length us, event | category | flops | bytes accessed | tf_op | source)
XLA Modules:
  0.0 170.0 jit_solution(4922173959408880749)
XLA Ops:
  0.6 1.3 reshape.22.gain_ref
  1.9 2.4 %copy.9 = bf16[1664,257]{1,0:T(8,128)(2,1)} copy(bf16[1664,257]{0,1:T(8,128)(2,1)} %bitcast.9) | data formatting | bytes 1710592 | tf_op jit(solution)/shard_map/transpose | solution.py:446
  4.3 52.5 %shard_map.84 = (bf16[257,1664]{1,0:T(8,128)(2,1)}, bf16[257,1664]{1,0:T(8,128)(2,1)}, bf16[3,16,104,257]{3,2,1,0:T(8,128)(2,1)}, bf16[257,1664]{1,0:T(8,128)(2,1)}, f32[8,1664]{1,0:T(8,128)}) custom-call(bf16[257,1664]{1,0:T(8,128)(2,1)} %bitcast.12, bf16[257,1664]{1,0:T(8,128)(2,1)} %bitcast.10, f32[1,1664]{1,0:T(1,128)} %reshape.22.gain_ref, ...), custom_call_target="tpu_custom_call" | custom-call | flops 12000000000 | bytes 27262976 | tf_op jit(solution)/shard_map/pallas_call | solution.py:110
  56.8 107.7 %shard_map.85 = (f32[208,1664]{1,0:T(8,128)}, f32[8,1664]{1,0:T(8,128)}) custom-call(bf16[48,104,257]{2,1,0:T(8,128)(2,1)} %bitcast.13, bf16[16,104,257]{2,1,0:T(8,128)(2,1)} %bitcast.8, bf16[257,1664]{1,0:T(8,128)(2,1)} %get-tuple-element.13.lno, bf16[257,1664]{1,0:T(8,128)(2,1)} %get-tuple-element.14.ao, f32[8,1664]{1,0:T(8,128)} %get-tuple-element.15.gain_in), custom_call_target="tpu_custom_call" | custom-call | flops 5692850176 | bytes 16777216 | tf_op jit(solution)/shard_map/pallas_call | solution.py:423
  164.5 1.4 multiply_reduce_fusion
  165.9 1.8 %slice.10 = f32[52,1664]{1,0:T(8,128)} slice(f32[208,1664]{1,0:T(8,128)} %get-tuple-element.16), slice={[156:208], [0:1664]} | slice | bytes 692224 | tf_op jit(solution)/shard_map/slice | solution.py:449
  167.7 2.3 %slice.9 = f32[156,1664]{1,0:T(8,128)} slice(f32[208,1664]{1,0:T(8,128)} %get-tuple-element.16), slice={[0:156], [0:1664]} | slice | bytes 2076672 | tf_op jit(solution)/shard_map/slice | solution.py:449
where the time goes:
time: 171 us; the launch traced here: 170 us
  Pallas kernels  160 us (94%)
  local copies, waits for them, and re-layouts  7.72 us (5%)
    pallas_call x1, Pallas kernels, reduce_call(): pl.pallas_call(functools.partial(reduce_kernel, factor), out_shape=(jax.S...  108 us
    pallas_call x1, Pallas kernels, front_call(): pl.pallas_call(functools.partial(front_kernel, dim ** (-0.5)), grid=(HEAD...  52.5 us
    slice x2, local copies, waits for them, and re-layouts, local(): return (grad_input[None], total[:Q_ROWS], total[Q_ROWS:], gain[0] * factor)  4.03 us

commit v1 on v0

v1 whole, which is shorter than its diff:
```python
import functools

import jax
import jax.numpy as jnp
from jax import lax
from jax.experimental import pallas as pl
from jax.experimental.pallas import tpu as pltpu
from jax.sharding import PartitionSpec as P

HEADS = 16


ln_epsilon = 1e-06


LANES = 128
WINDOW = 256


def dot(a, b, over=((1,), (0,))):
    return lax.dot_general(a, b, (over, ((), ())), preferred_element_type=jnp.float32)


def low(a):
    return a.astype(jnp.bfloat16)


def normalise(x_ref):
    x = x_ref[...].astype(jnp.float32)
    centered = x - jnp.mean(x, axis=-1, keepdims=True)
    inv_sigma = lax.rsqrt(jnp.mean(centered * centered, axis=-1, keepdims=True) + ln_epsilon)
    return centered * inv_sigma, inv_sigma


def front_kernel(scale, x_ref, cot_ref, gain_ref, w_ref, wo_ref,
                 lno_ref, ao_ref, gt_ref, gx_ref, gg_ref, wpad, gln):
    h = pl.program_id(0)
    dim = w_ref.shape[2]

    @pl.when(h == 0)
    def _():
        normed, _ = normalise(x_ref)
        lno_ref[...] = low(normed * gain_ref[...])
        wpad[...] = jnp.zeros_like(wpad)
        gln[...] = jnp.zeros_like(gln)

    for s in range(3):
        wpad[s * LANES : s * LANES + dim, :] = w_ref[s, 0]
    qkv = low(dot(lno_ref[...], wpad[...], ((1,), (1,))))
    q, k, v = (qkv[:, s * LANES : (s + 1) * LANES] for s in range(3))
    scores = dot(q, k, ((1,), (1,))) * scale
    expo = jnp.exp(scores - jnp.max(scores, axis=-1, keepdims=True))
    prob = expo / jnp.sum(expo, axis=-1, keepdims=True)
    prob_low = low(prob)

    start = jnp.minimum(lax.div(h * dim, LANES) * LANES, wo_ref.shape[1] - WINDOW)
    start = pl.multiple_of(start, LANES)
    offset = h * dim - start
    lane = lax.broadcasted_iota(jnp.int32, (1, WINDOW), 1)
    attn = dot(prob_low, v)
    attn = jnp.concatenate([attn, jnp.zeros_like(attn)], axis=1)
    attn = pltpu.roll(attn, offset, 1)
    window = ao_ref[:, pl.ds(start, WINDOW)].astype(jnp.float32)
    inside = jnp.logical_and(lane >= offset, lane < offset + dim)
    ao_ref[:, pl.ds(start, WINDOW)] = low(jnp.where(inside, attn, window))

    grad = dot(cot_ref[...], wo_ref[:, pl.ds(start, WINDOW)])
    grad = pltpu.roll(grad, lax.rem(WINDOW - offset, WINDOW), 1)[:, :LANES]
    grad = low(jnp.where(lane[:, :LANES] < dim, grad, 0.0))
    grad_prob = dot(grad, v, ((1,), (1,)))
    inner = jnp.sum(grad_prob * prob, axis=-1, keepdims=True)
    grad_score = low(prob * (grad_prob - inner) * scale)

    gq = low(dot(grad_score, k)).astype(jnp.float32)
    gkt = low(dot(q, grad_score, ((0,), (0,)))).astype(jnp.float32)
    gvt = low(dot(grad, prob_low, ((0,), (0,)))).astype(jnp.float32)
    gt_ref[0, 0] = low(gq.T[:dim])
    gt_ref[1, 0] = low(gkt[:dim])
    gt_ref[2, 0] = low(gvt[:dim])
    gcat = low(jnp.concatenate([gq, gkt.T, gvt.T], axis=1))
    gln[...] += dot(gcat, wpad[...])

    @pl.when(h == pl.num_programs(0) - 1)
    def _():
        normed, inv_sigma = normalise(x_ref)
        grad_ln = gln[...]
        total = jnp.sum(grad_ln * normed, axis=0, keepdims=True)
        row = lax.broadcasted_iota(jnp.int32, gg_ref.shape, 0)
        gg_ref[...] = jnp.where(row == 0, total, 0.0)
        g = grad_ln * gain_ref[...]
        grad_x = inv_sigma * (
            g - jnp.mean(g, axis=-1, keepdims=True) - normed * jnp.mean(g * normed, axis=-1, keepdims=True)
        )
        gx_ref[...] = low(cot_ref[...].astype(jnp.float32) + grad_x)


def front_call(x, cot, gain, w_qkv, w_out):
    tok, width = x.shape
    dim = width // HEADS
    whole = lambda a: pl.BlockSpec(a.shape, lambda h: (0,) * len(a.shape))
    w = w_qkv.reshape(3, HEADS, dim, width)
    gain = gain.reshape(1, width)
    outs = (
        jax.ShapeDtypeStruct((tok, width), jnp.bfloat16),
        jax.ShapeDtypeStruct((tok, width), jnp.bfloat16),
        jax.ShapeDtypeStruct((3, HEADS, dim, tok), jnp.bfloat16),
        jax.ShapeDtypeStruct((tok, width), jnp.bfloat16),
        jax.ShapeDtypeStruct((8, width), jnp.float32),
    )
    return pl.pallas_call(
        functools.partial(front_kernel, dim**-0.5),
        grid=(HEADS,),
        out_shape=outs,
        in_specs=[whole(x), whole(cot), whole(gain), pl.BlockSpec((3, 1, dim, width), lambda h: (0, h, 0, 0)), whole(w_out)],
        out_specs=[whole(outs[0]), whole(outs[1]), pl.BlockSpec((3, 1, dim, tok), lambda h: (0, h, 0, 0)), whole(outs[3]), whole(outs[4])],
        scratch_shapes=[pltpu.VMEM((3 * LANES, width), jnp.bfloat16), pltpu.VMEM((tok, width), jnp.float32)],
        compiler_params=pltpu.CompilerParams(vmem_limit_bytes=56 * 2**20, dimension_semantics=("arbitrary",)),
        cost_estimate=pl.CostEstimate(flops=12 * 10**9, bytes_accessed=26 * 2**20, transcendentals=HEADS * tok * tok),
    )(x, cot, gain, w, w_out)


BLOCKS = 32
ROWS = 208
Q_ROWS = 156
PARTS = ((0, 80), (80, 64), (144, 64))
CUTS = (48, 32, 32)
RING = 4
LAG = 2
MESH = pl.DeviceIdType.MESH


def rem(a, b):
    return lax.rem(a, jnp.int32(b))


def div(a, b):
    return lax.div(a, jnp.int32(b))


def column_halves(cols):
    edge = (cols // LANES + 1) // 2 * LANES
    return ((0, edge), (edge, cols))


def reduce_kernel(factor, gt, ct, lno, ao, gain_in, out, gain_out, G, sg, rg, *scratch):
    cols = lno.shape[1]
    spans = column_halves(cols)
    per = len(scratch) // 2
    sides = []
    for h in range(2):
        s = scratch[h * per : (h + 1) * per]
        sides.append(dict(S=s[0], R0=s[1], T0=s[2], halves=(s[3], s[6], s[9]), wholes=(s[4], s[7], s[10]),
                          later=(s[5], s[8], s[11]), C=s[12:15], T1=s[15], F=s[16], sems=s[17:27]))

    wide, narrow = lax.axis_index("wide"), lax.axis_index("narrow")
    xh, y, z = div(wide, 16), rem(div(wide, 4), 4), rem(wide, 4)
    xl, c = div(narrow, 2), rem(narrow, 2)
    x = 2 * xh + xl
    place = (x, y, z)

    def device(x_, y_, z_, c_):
        return (div(x_, 2) * 16 + y_ * 4 + z_, rem(x_, 2) * 2 + c_)

    def shift(dim, by):
        at = [x, y, z]
        at[dim] = rem(at[dim] + by, 4)
        return device(*at, c)

    mate = device(x, y, z, 1 - c)
    peers = [mate] + [shift(d, by) for d in range(3) for by in (1, 2, 3)]
    barrier = pltpu.get_barrier_semaphore()
    for peer in peers:
        pl.semaphore_signal(barrier, inc=1, device_id=peer, device_id_type=MESH)
    pl.semaphore_wait(barrier, len(peers))

    def remote(src, dst, ssem, rsem, to):
        return pltpu.make_async_remote_copy(src_ref=src, dst_ref=dst, send_sem=ssem, recv_sem=rsem,
                                            device_id=to, device_id_type=MESH)

    def accumulate(dst, *more):
        total = dst[...].astype(jnp.float32)
        for term in more:
            total = total + term[...].astype(jnp.float32)
        dst[...] = total.astype(jnp.bfloat16)

    rings = ((2, c, lambda r: mate), (4, x, lambda r: shift(0, r)), (4, y, lambda r: shift(1, r)), (4, z, lambda r: shift(2, r)))
    gain_copies = []

    def gain_start(k):
        n, m, to = rings[k]
        G[k, m] = gain_out[...] if k else gain_in[...]
        for r in range(n - 1):
            copy = remote(G.at[k, m], G.at[k, m], sg.at[k, r], rg.at[k, r], to(r + 1))
            copy.start()
            gain_copies.append(copy)

    def gain_end(k):
        while gain_copies:
            gain_copies.pop().wait()
        total = G[k, 0]
        for other in range(1, rings[k][0]):
            total = total + G[k, other]
        gain_out[...] = total

    def rows_of_pair(b):
        g = jnp.concatenate([gt[3 * b + i].astype(jnp.float32) for i in range(3)], axis=0)
        d = ct[b].astype(jnp.float32)
        out_rows = ROWS - Q_ROWS
        return tuple(
            jnp.concatenate([g[i * Q_ROWS : (i + 1) * Q_ROWS], d[i * out_rows : (i + 1) * out_rows]], axis=0)
            for i in range(2)
        )

    def product(left, right, lo, hi):
        full = right.shape[0] // 256 * 256
        total = dot(low(left[:, :full]), right[0:full, lo:hi])
        for k in range(full, right.shape[0]):
            total = total + left[:, k : k + 1] * right[k : k + 1, lo:hi].astype(jnp.float32)
        return total * factor

    def fill(side, span, b, slot):
        even, odd = rows_of_pair(b)
        mine_odd = rem(c + div(b, 8) + rem(div(b, 2), 4), 2) == 1
        give, keep = jnp.where(mine_odd, even, odd), jnp.where(mine_odd, odd, even)
        first = jnp.concatenate([give[0:160], keep[0:160]], axis=0)
        last = jnp.concatenate([give[144:208], keep[144:208]], axis=0)
        row = lax.broadcasted_iota(jnp.int32, (16, 1), 0)
        width = span[1] - span[0]
        for lo in range(0, width, 512):
            hi = min(width, lo + 512)
            p = product(first, lno, span[0] + lo, span[0] + hi)
            q = product(last, ao, span[0] + lo, span[0] + hi)
            for k, dst, at in ((0, side["T0"], slot), (1, side["S"], b)):
                u, v = p[160 * k : 160 * k + 160], q[64 * k : 64 * k + 64]
                dst[at, 0:144, lo:hi] = low(u[0:144])
                dst[at, 144:160, lo:hi] = low(jnp.where(row < Q_ROWS - 144, u[144:160], v[0:16]))
                dst[at, 160:208, lo:hi] = low(v[16:64])

    def core_copy(side, b, slot):
        return remote(side["T0"].at[slot], side["R0"].at[b], side["sems"][0].at[b], side["sems"][1].at[b], mate)

    def produce(h):
        side = sides[h]

        @pl.loop(0, 16 + LAG)
        def _(n):
            @pl.when(n < 16)
            def _():
                slot = rem(n, RING)

                @pl.when(n >= RING)
                def _():
                    core_copy(side, n - RING, slot).wait_send()

                fill(side, spans[h], n, slot)
                core_copy(side, n, slot).start()

            @pl.when(n >= LAG)
            def _():
                b = n - LAG
                core_copy(side, b, 0).wait_recv()
                accumulate(side["S"].at[b], side["R0"].at[b])

        for n in range(16 - RING, 16):
            core_copy(side, n, n % RING).wait_send()

    orders = ((1, 2, 0), (2, 0, 1), (0, 1, 2))
    firsts = (
        lambda t, i: (i // 2) * 8 + t * 2 + i % 2,
        lambda t, i: (i // 2) * 8 + (2 * (i % 2) + rem(c + t + i // 2, 2)) * 2 + div(t, 2),
        lambda t, i: div(t, 2) * 8 + i * 2 + rem(t, 2),
    )
    seconds = (
        lambda t: (rem(c + y + t, 2) * 8 + y * 2 + div(t, 2), rem(c + y + t, 2) * 2 + div(t, 2)),
        lambda t: (div(t, 2) * 8 + (2 * rem(t, 2) + rem(c + z + div(t, 2), 2)) * 2 + div(z, 2), t),
        lambda t: (div(x, 2) * 8 + t * 2 + rem(x, 2), t),
    )

    def part(h, p, b):
        return sides[h]["S"].at[b, pl.ds(*PARTS[p]), :]

    def half_copy(h, p, to, i, src):
        sems = sides[h]["sems"]
        return remote(src, sides[h]["halves"][p].at[to, i], sems[2].at[p, to, i], sems[3].at[p, to, i],
                      shift(orders[p][0], 1 + 2 * to))

    def whole_copy(h, p, to, i, src):
        sems = sides[h]["sems"]
        return remote(src, sides[h]["wholes"][p].at[to, i], sems[4].at[p, to, i], sems[5].at[p, to, i],
                      shift(orders[p][0], 1 + 2 * to))

    six = [(p, to) for to in range(2) for p in range(3)]

    def first_sends(h):
        for i in range(2):
            for p, to in six:
                t = rem(place[orders[p][0]] + 2, 4)
                half_copy(h, p, to, i, part(h, p, firsts[p](t, i + 2 * to))).start()
        for i in range(2):
            for p, to in six:
                t = rem(place[orders[p][0]] + 1 + 2 * to, 4)
                index = i + 2 - 2 * to
                whole_copy(h, p, to, index, part(h, p, firsts[p](t, index))).start()

    def first_relays(h):
        for i in range(2):
            for p, to in six:
                halves = sides[h]["halves"][p]
                half_copy(h, p, to, i, halves.at[to, i]).wait_recv()
                t = rem(place[orders[p][0]] + 1 + 2 * to, 4)
                index = i + 2 * to
                block = part(h, p, firsts[p](t, index))
                accumulate(block, halves.at[to, i])
                whole_copy(h, p, to, index, block).start()

    def ready(h, p, t):
        b, i = seconds[p](t)
        wholes = sides[h]["wholes"][p]
        for to in range(2):
            whole_copy(h, p, to, i, wholes.at[to, i]).wait_recv()
        accumulate(part(h, p, b), wholes.at[0, i], wholes.at[1, i])
        return part(h, p, b)

    def second_copy(h, p, k, what):
        edge = CUTS[p]
        lower, upper = pl.ds(0, edge), pl.ds(edge, PARTS[p][1] - edge)
        rows, slot, by = ((lower, 0, 1), (upper, 0, 3), (upper, 1, 1), (lower, 2, 3), (lower, 1, 1), (upper, 2, 3))[k]
        sems = sides[h]["sems"]
        return remote(what.at[rows], sides[h]["later"][p].at[slot, rows], sems[6].at[p, k], sems[7].at[p, k],
                      shift(orders[p][1], by))

    def block2(h, p, by):
        return part(h, p, seconds[p](rem(place[orders[p][1]] + by, 4))[0])

    def second_sends(h):
        for p in range(3):
            opposite = ready(h, p, rem(place[orders[p][1]] + 2, 4))
            second_copy(h, p, 0, opposite).start()
            second_copy(h, p, 1, opposite).start()
        for p in range(3):
            second_copy(h, p, 2, ready(h, p, rem(place[orders[p][1]] + 1, 4))).start()
            second_copy(h, p, 3, ready(h, p, rem(place[orders[p][1]] + 3, 4))).start()

    def second_relays(h):
        for p in range(3):
            edge = CUTS[p]
            inbox = sides[h]["later"][p]
            for k, by, rows in ((0, 1, pl.ds(0, edge)), (1, 3, pl.ds(edge, PARTS[p][1] - edge))):
                what = block2(h, p, by)
                second_copy(h, p, k, what).wait_recv()
                accumulate(what.at[rows], inbox.at[0, rows])
                second_copy(h, p, 4 + k, what).start()
        for p in range(3):
            ready(h, p, place[orders[p][1]])

    chosen = c == rem(xh + y + z, 2)
    partner = device(2 * xh + 1 - xl, y, z, c)
    outward = device(rem(x + 3 + 2 * xl, 4), y, z, c)
    y_to = 2 * xl + rem(c + z + xh, 2)
    z_to = 2 * xl + rem(c + y + xh, 2)
    reach = ((1, 2, y_to, y, lambda: device(x, y_to, z, c)), (2, 5, z_to, z, lambda: device(x, y, z_to, c)))

    def third(h, src, dst, k, to):
        sems = sides[h]["sems"]
        return remote(src, dst, sems[8].at[k], sems[9].at[k], to)

    def mine(h, p):
        return block2(h, p, 0)

    def final(h, p):
        return sides[h]["F"].at[pl.ds(*PARTS[p]), :]

    def to_pair(h):
        return third(h, mine(h, 0), sides[h]["C"][0].at[0], 0, outward)

    def swap(h):
        return third(h, sides[h]["T1"], sides[h]["C"][0].at[1], 1, partner)

    def share(h, p):
        return third(h, final(h, p), final(h, p), 7 + p, partner)

    def hand(h):
        return third(h, sides[h]["F"], sides[h]["F"], 10, mate)

    def third_sends(h):
        for p in range(3):
            for k in range(2, 6):
                second_copy(h, p, k, mine(h, p)).wait_recv()
            accumulate(mine(h, p), sides[h]["later"][p].at[1], sides[h]["later"][p].at[2])
            if p == 0:
                @pl.when(jnp.logical_not(chosen))
                def _():
                    to_pair(h).start()
            else:
                _, base, to, at, where = reach[p - 1]
                for r in range(3):
                    @pl.when(rem(at - to + 4, 4) == r + 1)
                    def _():
                        third(h, mine(h, p), sides[h]["C"][p].at[r], base + r, where()).start()

    def third_sums(h):
        side = sides[h]

        @pl.when(chosen)
        def _():
            to_pair(h).wait_recv()
            side["T1"][...] = low(mine(h, 0)[...].astype(jnp.float32) + side["C"][0][0].astype(jnp.float32))
            swap(h).start()

        for p, base, to, at, where in reach:
            @pl.when(at == to)
            def _():
                total = mine(h, p)[...].astype(jnp.float32)
                for r in range(3):
                    third(h, mine(h, p), side["C"][p].at[r], base + r, mate).wait_recv()
                    total = total + side["C"][p][r].astype(jnp.float32)
                final(h, p)[...] = low(total)
                share(h, p).start()

    def finish(h):
        side = sides[h]

        @pl.when(chosen)
        def _():
            swap(h).wait_recv()
            final(h, 0)[...] = low(side["T1"][...].astype(jnp.float32) + side["C"][0][1].astype(jnp.float32))

        for p, base, to, at, where in reach:
            @pl.when(jnp.logical_and(chosen, at != to))
            def _():
                share(h, p).wait_recv()

        @pl.when(chosen)
        def _():
            hand(h).start()

    def write(h):
        @pl.when(jnp.logical_not(chosen))
        def _():
            hand(h).wait_recv()

        out[:, spans[h][0] : spans[h][1]] = sides[h]["F"][...].astype(jnp.float32)

    def drain(h):
        for p in range(3):
            for to in range(2):
                for i in range(4):
                    whole_copy(h, p, to, i, sides[h]["wholes"][p].at[to, i]).wait_send()
                for i in range(2):
                    half_copy(h, p, to, i, sides[h]["halves"][p].at[to, i]).wait_send()
            for k in range(6):
                second_copy(h, p, k, mine(h, p)).wait_send()

        @pl.when(chosen)
        def _():
            swap(h).wait_send()
            hand(h).wait_send()

        @pl.when(jnp.logical_not(chosen))
        def _():
            to_pair(h).wait_send()

        for p, base, to, at, where in reach:
            @pl.when(at == to)
            def _():
                share(h, p).wait_send()

            for r in range(3):
                @pl.when(rem(at - to + 4, 4) == r + 1)
                def _():
                    third(h, mine(h, p), sides[h]["C"][p].at[r], base + r, where()).wait_send()

    produce(0)
    first_sends(0)
    produce(1)
    first_relays(0)
    first_sends(1)
    gain_start(0)
    second_sends(0)
    gain_end(0)
    gain_start(1)
    first_relays(1)
    gain_end(1)
    gain_start(2)
    second_relays(0)
    second_sends(1)
    third_sends(0)
    gain_end(2)
    gain_start(3)
    second_relays(1)
    third_sums(0)
    third_sends(1)
    finish(0)
    gain_end(3)
    third_sums(1)
    write(0)
    finish(1)
    write(1)
    drain(0)
    drain(1)


def reduce_call(gt, ct, lno, ao, gain, factor):
    cols = lno.shape[1]
    dma = pltpu.SemaphoreType.DMA
    vm = pl.BlockSpec(memory_space=pltpu.VMEM)
    scratch = [pltpu.VMEM((4, 4) + gain.shape, jnp.float32), dma((4, 3)), dma((4, 3))]
    for lo, hi in column_halves(cols):
        bf = lambda *shape: pltpu.VMEM(shape + (hi - lo,), jnp.bfloat16)
        sizes = [size for _, size in PARTS]
        scratch += [bf(16, ROWS), bf(16, ROWS), bf(RING, ROWS)]
        scratch += [x for s in sizes for x in (bf(2, 2, s), bf(2, 4, s), bf(3, s))]
        scratch += [bf(2, sizes[0]), bf(3, sizes[1]), bf(3, sizes[2]), bf(sizes[0]), bf(ROWS)]
        scratch += [dma((16,))] * 2 + [dma((3, 2, 2))] * 2 + [dma((3, 2, 4))] * 2 + [dma((3, 6))] * 2 + [dma((11,))] * 2
    return pl.pallas_call(
        functools.partial(reduce_kernel, factor),
        out_shape=(jax.ShapeDtypeStruct((ROWS, cols), jnp.float32), jax.ShapeDtypeStruct(gain.shape, jnp.float32)),
        in_specs=[vm] * 5,
        out_specs=[vm] * 2,
        scratch_shapes=scratch,
        compiler_params=pltpu.CompilerParams(collective_id=0, has_side_effects=True, vmem_limit_bytes=62 * 2**20),
        cost_estimate=pl.CostEstimate(flops=2 * BLOCKS * ROWS * lno.shape[0] * cols, bytes_accessed=2**24, transcendentals=0),
    )(gt, ct, lno, ao, gain)


def local(tokens, cotangent, ln_gain, w_qkv, w_out):
    images = tokens.shape[0] * lax.axis_size("wide") * lax.axis_size("narrow")
    factor = 1.0 / images
    x, cot = tokens[0], cotangent[0]
    ln_out, attn_out, grad_t, grad_input, gain = front_call(x, cot, ln_gain, w_qkv, w_out)
    cot_t = cot.T.reshape(BLOCKS // 2, -1, cot.shape[0])
    width = cot.shape[1]
    gain = jnp.zeros((16, LANES), jnp.float32).at[: width // LANES].set(gain[0].reshape(-1, LANES))
    grad_t = grad_t.reshape(BLOCKS * 3 // 2, -1, cot.shape[0])
    total, gain = reduce_call(grad_t, cot_t, ln_out, attn_out, gain, factor)
    return (grad_input[None], total[:Q_ROWS], total[Q_ROWS:], gain[: width // LANES].reshape(width) * factor)


def solution(mesh):
    return jax.shard_map(
        local,
        mesh=mesh,
        in_specs=(
            P(("wide", "narrow"), None, None),
            P(("wide", "narrow"), None, None),
            P(),
            P(),
            P(),
        ),
        out_specs=(P(("wide", "narrow"), None, None), P("wide", None), P("wide", None), P()),
        check_vma=False,
    )
```

time: 171 us -> 149 us (0.87)
  Pallas kernels: 160 us -> 138 us
    pallas_call x1, Pallas kernels: 108 us -> 85.1 us  [reduce_call(): pl.pallas_call(functools.partial(reduce_kernel, factor), out_shape=(jax.S...]
    slice x2 -> x3, local copies, waits for them, and re-layouts: 4.03 us -> 4.86 us  [the longest x1 2.27 us: local(): total[:Q_ROWS]]
where the time goes in v1:
time: 149 us
  Pallas kernels  138 us (93%)
  local copies, waits for them, and re-layouts  9.16 us (6%)
    pallas_call x1, Pallas kernels, reduce_call(): pl.pallas_call(functools.partial(reduce_kernel, factor), out_shape=(jax.S...  85.1 us
    pallas_call x1, Pallas kernels, front_call(): pl.pallas_call(functools.partial(front_kernel, dim ** (-0.5)), grid=(HEAD...  52.5 us

profile of v1, /device:TPU:1, one launch (start us, length us, event | category | flops | bytes accessed | tf_op | source)
XLA Modules:
  0.0 148.7 jit_solution(8655486791222275560)
XLA Ops:
  0.6 1.3 reshape.51.gain_ref
  1.9 2.4 %copy.9 = bf16[1664,257]{1,0:T(8,128)(2,1)} copy(bf16[1664,257]{0,1:T(8,128)(2,1)} %bitcast.12) | data formatting | bytes 1710592 | tf_op jit(solution)/shard_map/transpose | solution.py:531
  4.3 52.5 %shard_map.84 = (bf16[257,1664]{1,0:T(8,128)(2,1)}, bf16[257,1664]{1,0:T(8,128)(2,1)}, bf16[3,16,104,257]{3,2,1,0:T(8,128)(2,1)}, bf16[257,1664]{1,0:T(8,128)(2,1)}, f32[8,1664]{1,0:T(8,128)}) custom-call(bf16[257,1664]{1,0:T(8,128)(2,1)} %bitcast.16, bf16[257,1664]{1,0:T(8,128)(2,1)} %bitcast.13, f32[1,1664]{1,0:T(1,128)} %reshape.51.gain_ref, ...), custom_call_target="tpu_custom_call" | custom-call | flops 12000000000 | bytes 27262976 | tf_op jit(solution)/shard_map/pallas_call | solution.py:110
  56.8 0.8 slice_reduce_fusion
  57.6 0.6 scatter.4.gain_in
  58.3 85.1 %shard_map.85 = (f32[208,1664]{1,0:T(8,128)}, f32[16,128]{1,0:T(8,128)}) custom-call(bf16[48,104,257]{2,1,0:T(8,128)(2,1)} %bitcast.17, bf16[16,104,257]{2,1,0:T(8,128)(2,1)} %bitcast.11, bf16[257,1664]{1,0:T(8,128)(2,1)} %get-tuple-element.25.lno, bf16[257,1664]{1,0:T(8,128)(2,1)} %get-tuple-element.26.ao, f32[16,128]{1,0:T(8,128)} %scatter.4.gain_in), custom_call_target="tpu_custom_call" | custom-call | flops 5692850176 | bytes 16777216 | tf_op jit(solution)/shard_map/pallas_call | solution.py:515
  143.3 1.3 multiply_bitcast_fusion
  144.6 1.8 %slice.30 = f32[52,1664]{1,0:T(8,128)} slice(f32[208,1664]{1,0:T(8,128)} %get-tuple-element.28), slice={[156:208], [0:1664]} | slice | bytes 692224 | tf_op jit(solution)/shard_map/slice | solution.py:536
  146.4 2.3 %slice.29 = f32[156,1664]{1,0:T(8,128)} slice(f32[208,1664]{1,0:T(8,128)} %get-tuple-element.28), slice={[0:156], [0:1664]} | slice | bytes 2076672 | tf_op jit(solution)/shard_map/slice | solution.py:536

commit v2 on v1

--- a/solution.py
+++ b/solution.py
@@ -33,16 +33,15 @@
 
 
 def front_kernel(scale, x_ref, cot_ref, gain_ref, w_ref, wo_ref,
-                 lno_ref, ao_ref, gt_ref, gx_ref, gg_ref, wpad, gln):
+                 lno_ref, ao_ref, gt_ref, wpad):
     h = pl.program_id(0)
     dim = w_ref.shape[2]
 
     @pl.when(h == 0)
     def _():
         normed, _ = normalise(x_ref)
-        lno_ref[...] = low(normed * gain_ref[...])
+        lno_ref[...] = low(normed * gain_ref[...].reshape(1, -1))
         wpad[...] = jnp.zeros_like(wpad)
-        gln[...] = jnp.zeros_like(gln)
 
     for s in range(3):
         wpad[s * LANES : s * LANES + dim, :] = w_ref[s, 0]
@@ -71,27 +70,9 @@
     inner = jnp.sum(grad_prob * prob, axis=-1, keepdims=True)
     grad_score = low(prob * (grad_prob - inner) * scale)
 
-    gq = low(dot(grad_score, k)).astype(jnp.float32)
-    gkt = low(dot(q, grad_score, ((0,), (0,)))).astype(jnp.float32)
-    gvt = low(dot(grad, prob_low, ((0,), (0,)))).astype(jnp.float32)
-    gt_ref[0, 0] = low(gq.T[:dim])
-    gt_ref[1, 0] = low(gkt[:dim])
-    gt_ref[2, 0] = low(gvt[:dim])
-    gcat = low(jnp.concatenate([gq, gkt.T, gvt.T], axis=1))
-    gln[...] += dot(gcat, wpad[...])
-
-    @pl.when(h == pl.num_programs(0) - 1)
-    def _():
-        normed, inv_sigma = normalise(x_ref)
-        grad_ln = gln[...]
-        total = jnp.sum(grad_ln * normed, axis=0, keepdims=True)
-        row = lax.broadcasted_iota(jnp.int32, gg_ref.shape, 0)
-        gg_ref[...] = jnp.where(row == 0, total, 0.0)
-        g = grad_ln * gain_ref[...]
-        grad_x = inv_sigma * (
-            g - jnp.mean(g, axis=-1, keepdims=True) - normed * jnp.mean(g * normed, axis=-1, keepdims=True)
-        )
-        gx_ref[...] = low(cot_ref[...].astype(jnp.float32) + grad_x)
+    gt_ref[0, 0] = low(dot(grad_score, k).T[:dim])
+    gt_ref[1, 0] = low(dot(q, grad_score, ((0,), (0,)))[:dim])
+    gt_ref[2, 0] = low(dot(grad, prob_low, ((0,), (0,)))[:dim])
 
 
 def front_call(x, cot, gain, w_qkv, w_out):
@@ -99,21 +80,18 @@
     dim = width // HEADS
     whole = lambda a: pl.BlockSpec(a.shape, lambda h: (0,) * len(a.shape))
     w = w_qkv.reshape(3, HEADS, dim, width)
-    gain = gain.reshape(1, width)
     outs = (
         jax.ShapeDtypeStruct((tok, width), jnp.bfloat16),
         jax.ShapeDtypeStruct((tok, width), jnp.bfloat16),
         jax.ShapeDtypeStruct((3, HEADS, dim, tok), jnp.bfloat16),
-        jax.ShapeDtypeStruct((tok, width), jnp.bfloat16),
-        jax.ShapeDtypeStruct((8, width), jnp.float32),
     )
     return pl.pallas_call(
         functools.partial(front_kernel, dim**-0.5),
         grid=(HEADS,),
         out_shape=outs,
         in_specs=[whole(x), whole(cot), whole(gain), pl.BlockSpec((3, 1, dim, width), lambda h: (0, h, 0, 0)), whole(w_out)],
-        out_specs=[whole(outs[0]), whole(outs[1]), pl.BlockSpec((3, 1, dim, tok), lambda h: (0, h, 0, 0)), whole(outs[3]), whole(outs[4])],
-        scratch_shapes=[pltpu.VMEM((3 * LANES, width), jnp.bfloat16), pltpu.VMEM((tok, width), jnp.float32)],
+        out_specs=[whole(outs[0]), whole(outs[1]), pl.BlockSpec((3, 1, dim, tok), lambda h: (0, h, 0, 0))],
+        scratch_shapes=[pltpu.VMEM((3 * LANES, width), jnp.bfloat16)],
         compiler_params=pltpu.CompilerParams(vmem_limit_bytes=56 * 2**20, dimension_semantics=("arbitrary",)),
         cost_estimate=pl.CostEstimate(flops=12 * 10**9, bytes_accessed=26 * 2**20, transcendentals=HEADS * tok * tok),
     )(x, cot, gain, w, w_out)
@@ -142,7 +120,8 @@
     return ((0, edge), (edge, cols))
 
 
-def reduce_kernel(factor, gt, ct, lno, ao, gain_in, out, gain_out, G, sg, rg, *scratch):
+def reduce_kernel(factor, gt, ct, lno, ao, x_ref, cot_ref, gain_ref, w_hbm, qkv_out, out_out, gain_out, gx_ref,
+                  G, sg, rg, wbuf, wpad, gln, row, wsem, *scratch):
     cols = lno.shape[1]
     spans = column_halves(cols)
     per = len(scratch) // 2
@@ -188,19 +167,63 @@
 
     def gain_start(k):
         n, m, to = rings[k]
-        G[k, m] = gain_out[...] if k else gain_in[...]
+        if k == 0:
+            G[k, m] = jnp.zeros(G.shape[2:], jnp.float32)
+            for i in range(cols // LANES):
+                G[k, m, i : i + 1, :] = row[:, i * LANES : (i + 1) * LANES]
+        else:
+            G[k, m] = gain_total(k - 1)
         for r in range(n - 1):
             copy = remote(G.at[k, m], G.at[k, m], sg.at[k, r], rg.at[k, r], to(r + 1))
             copy.start()
             gain_copies.append(copy)
 
+    def gain_total(k):
+        total = G[k, 0]
+        for other in range(1, rings[k][0]):
+            total = total + G[k, other]
+        return total
+
     def gain_end(k):
         while gain_copies:
             gain_copies.pop().wait()
-        total = G[k, 0]
-        for other in range(1, rings[k][0]):
-            total = total + G[k, other]
-        gain_out[...] = total
+        if k == 3:
+            total = gain_total(k) * factor
+            for i in range(cols // LANES):
+                gain_out[:, i * LANES : (i + 1) * LANES] = total[i : i + 1]
+
+    def weights(h, slot):
+        return pltpu.make_async_copy(w_hbm.at[:, h], wbuf.at[slot], wsem.at[slot])
+
+    def input_gradient():
+        dim = gt.shape[1]
+        gln[...] = jnp.zeros_like(gln)
+        wpad[...] = jnp.zeros_like(wpad)
+
+        @pl.loop(0, HEADS)
+        def _(h):
+            slot = rem(h, 2)
+            weights(h, slot).wait()
+
+            @pl.when(h < HEADS - 1)
+            def _():
+                weights(h + 1, 1 - slot).start()
+
+            pad = jnp.zeros((LANES - dim, gt.shape[2]), jnp.float32)
+            stack = []
+            for s in range(3):
+                wpad[s * LANES : s * LANES + dim, :] = wbuf[slot, s]
+                stack += [gt[s * HEADS + h].astype(jnp.float32), pad]
+            gln[...] += dot(low(jnp.concatenate(stack, axis=0).T), wpad[...])
+
+        normed, inv_sigma = normalise(x_ref)
+        grad_ln = gln[...]
+        row[...] = jnp.sum(grad_ln * normed, axis=0, keepdims=True)
+        g = grad_ln * gain_ref[...].reshape(1, -1)
+        grad_x = inv_sigma * (
+            g - jnp.mean(g, axis=-1, keepdims=True) - normed * jnp.mean(g * normed, axis=-1, keepdims=True)
+        )
+        gx_ref[...] = low(cot_ref[...].astype(jnp.float32) + grad_x)
 
     def rows_of_pair(b):
         g = jnp.concatenate([gt[3 * b + i].astype(jnp.float32) for i in range(3)], axis=0)
@@ -224,7 +247,7 @@
         give, keep = jnp.where(mine_odd, even, odd), jnp.where(mine_odd, odd, even)
         first = jnp.concatenate([give[0:160], keep[0:160]], axis=0)
         last = jnp.concatenate([give[144:208], keep[144:208]], axis=0)
-        row = lax.broadcasted_iota(jnp.int32, (16, 1), 0)
+        line = lax.broadcasted_iota(jnp.int32, (16, 1), 0)
         width = span[1] - span[0]
         for lo in range(0, width, 512):
             hi = min(width, lo + 512)
@@ -233,7 +256,7 @@
             for k, dst, at in ((0, side["T0"], slot), (1, side["S"], b)):
                 u, v = p[160 * k : 160 * k + 160], q[64 * k : 64 * k + 64]
                 dst[at, 0:144, lo:hi] = low(u[0:144])
-                dst[at, 144:160, lo:hi] = low(jnp.where(row < Q_ROWS - 144, u[144:160], v[0:16]))
+                dst[at, 144:160, lo:hi] = low(jnp.where(line < Q_ROWS - 144, u[144:160], v[0:16]))
                 dst[at, 160:208, lo:hi] = low(v[16:64])
 
     def core_copy(side, b, slot):
@@ -439,7 +462,9 @@
         def _():
             hand(h).wait_recv()
 
-        out[:, spans[h][0] : spans[h][1]] = sides[h]["F"][...].astype(jnp.float32)
+        total = sides[h]["F"][...].astype(jnp.float32)
+        qkv_out[:, spans[h][0] : spans[h][1]] = total[:Q_ROWS]
+        out_out[:, spans[h][0] : spans[h][1]] = total[Q_ROWS:]
 
     def drain(h):
         for p in range(3):
@@ -470,11 +495,13 @@
                 def _():
                     third(h, mine(h, p), sides[h]["C"][p].at[r], base + r, where()).wait_send()
 
+    weights(0, 0).start()
     produce(0)
     first_sends(0)
     produce(1)
     first_relays(0)
     first_sends(1)
+    input_gradient()
     gain_start(0)
     second_sends(0)
     gain_end(0)
@@ -500,11 +527,16 @@
     drain(1)
 
 
-def reduce_call(gt, ct, lno, ao, gain, factor):
-    cols = lno.shape[1]
+def reduce_call(gt, ct, lno, ao, x, cot, gain, w, factor):
+    tok, cols = lno.shape
     dma = pltpu.SemaphoreType.DMA
     vm = pl.BlockSpec(memory_space=pltpu.VMEM)
-    scratch = [pltpu.VMEM((4, 4) + gain.shape, jnp.float32), dma((4, 3)), dma((4, 3))]
+    dim = gt.shape[1]
+    scratch = [
+        pltpu.VMEM((4, 4, 16, LANES), jnp.float32), dma((4, 3)), dma((4, 3)),
+        pltpu.VMEM((2, 3, dim, cols), jnp.bfloat16), pltpu.VMEM((3 * LANES, cols), jnp.bfloat16),
+        pltpu.VMEM((tok, cols), jnp.float32), pltpu.VMEM((1, cols), jnp.float32), dma((2,)),
+    ]
     for lo, hi in column_halves(cols):
         bf = lambda *shape: pltpu.VMEM(shape + (hi - lo,), jnp.bfloat16)
         sizes = [size for _, size in PARTS]
@@ -514,26 +546,30 @@
         scratch += [dma((16,))] * 2 + [dma((3, 2, 2))] * 2 + [dma((3, 2, 4))] * 2 + [dma((3, 6))] * 2 + [dma((11,))] * 2
     return pl.pallas_call(
         functools.partial(reduce_kernel, factor),
-        out_shape=(jax.ShapeDtypeStruct((ROWS, cols), jnp.float32), jax.ShapeDtypeStruct(gain.shape, jnp.float32)),
-        in_specs=[vm] * 5,
-        out_specs=[vm] * 2,
+        out_shape=(
+            jax.ShapeDtypeStruct((Q_ROWS, cols), jnp.float32),
+            jax.ShapeDtypeStruct((ROWS - Q_ROWS, cols), jnp.float32),
+            jax.ShapeDtypeStruct((1, cols), jnp.float32),
+            jax.ShapeDtypeStruct((tok, cols), jnp.bfloat16),
+        ),
+        in_specs=[vm] * 7 + [pl.BlockSpec(memory_space=pl.ANY)],
+        out_specs=[vm] * 4,
         scratch_shapes=scratch,
-        compiler_params=pltpu.CompilerParams(collective_id=0, has_side_effects=True, vmem_limit_bytes=62 * 2**20),
-        cost_estimate=pl.CostEstimate(flops=2 * BLOCKS * ROWS * lno.shape[0] * cols, bytes_accessed=2**24, transcendentals=0),
-    )(gt, ct, lno, ao, gain)
+        compiler_params=pltpu.CompilerParams(collective_id=0, has_side_effects=True, vmem_limit_bytes=63 * 2**20),
+        cost_estimate=pl.CostEstimate(flops=2 * BLOCKS * ROWS * tok * cols, bytes_accessed=2**24, transcendentals=0),
+    )(gt, ct, lno, ao, x, cot, gain, w)
 
 
 def local(tokens, cotangent, ln_gain, w_qkv, w_out):
     images = tokens.shape[0] * lax.axis_size("wide") * lax.axis_size("narrow")
     factor = 1.0 / images
     x, cot = tokens[0], cotangent[0]
-    ln_out, attn_out, grad_t, grad_input, gain = front_call(x, cot, ln_gain, w_qkv, w_out)
+    ln_out, attn_out, grad_t = front_call(x, cot, ln_gain, w_qkv, w_out)
     cot_t = cot.T.reshape(BLOCKS // 2, -1, cot.shape[0])
-    width = cot.shape[1]
-    gain = jnp.zeros((16, LANES), jnp.float32).at[: width // LANES].set(gain[0].reshape(-1, LANES))
     grad_t = grad_t.reshape(BLOCKS * 3 // 2, -1, cot.shape[0])
-    total, gain = reduce_call(grad_t, cot_t, ln_out, attn_out, gain, factor)
-    return (grad_input[None], total[:Q_ROWS], total[Q_ROWS:], gain[: width // LANES].reshape(width) * factor)
+    w = w_qkv.reshape(3, HEADS, -1, cot.shape[1])
+    grad_qkv, grad_out, gain, grad_input = reduce_call(grad_t, cot_t, ln_out, attn_out, x, cot, ln_gain, w, factor)
+    return (grad_input[None], grad_qkv, grad_out, gain.reshape(-1))
 
 
 def solution(mesh):

time: 149 us -> 140 us (0.940)
  Pallas kernels: 138 us -> 130 us
  local copies, waits for them, and re-layouts: 9.16 us -> 7.57 us
    pallas_call x1, Pallas kernels: 52.5 us -> 40.4 us  [front_call(): pl.pallas_call(functools.partial(front_kernel, dim ** (-0.5)), grid=(HEAD...]
    unnamed x0 -> x5, local copies, waits for them, and re-layouts: none -> 5.15 us
    slice x3 -> x0, local copies, waits for them, and re-layouts: 4.86 us -> none  [the longest x1 2.27 us: local(): total[:Q_ROWS]]
    pallas_call x1, Pallas kernels: 85.1 us -> 89.3 us  [reduce_call(): pl.pallas_call(functools.partial(reduce_kernel, factor), out_shape=(jax.S...]
    transpose x1 -> x0, local copies, waits for them, and re-layouts: 2.4 us -> none  [local(): cot_t = cot.T.reshape(BLOCKS // 2, -1, cot.shape[0])]
where the time goes in v2:
time: 140 us; the launch traced here: 139 us
  Pallas kernels  130 us (93%)
  local copies, waits for them, and re-layouts  7.57 us (5%)
    pallas_call x1, Pallas kernels, reduce_call(): pl.pallas_call(functools.partial(reduce_kernel, factor), out_shape=(jax.S...  89.3 us
    pallas_call x1, Pallas kernels, front_call(): pl.pallas_call(functools.partial(front_kernel, dim ** (-0.5)), grid=(HEAD...  40.4 us
    unnamed x5, local copies, waits for them, and re-layouts  5.15 us

profile of v2, /device:TPU:1, one launch (start us, length us, event | category | flops | bytes accessed | tf_op | source)
XLA Modules:
  0.0 139.2 jit_solution(6465289737992618728)
XLA Ops:
  0.6 2.4 %copy.10 = bf16[1664,257]{1,0:T(8,128)(2,1)} copy(bf16[1664,257]{0,1:T(8,128)(2,1)} %bitcast.12) | data formatting | bytes 1710592 | tf_op jit(solution)/shard_map/reshape | solution.py:568
  3.0 40.4 %shard_map.84 = (bf16[257,1664]{1,0:T(8,128)(2,1)}, bf16[257,1664]{1,0:T(8,128)(2,1)}, bf16[3,16,104,257]{3,2,1,0:T(8,128)(2,1)}) custom-call(bf16[257,1664]{1,0:T(8,128)(2,1)} %bitcast.16, bf16[257,1664]{1,0:T(8,128)(2,1)} %bitcast.13, f32[1664]{0:T(1024)} %gain_ref.3, bf16[3,16,104,1664]{3,2,1,0:T(8,128)(2,1)} %bitcast.8, bf16[1664,1664]{1,0:T(8,128)(2,1)} %wo_ref.1), custom_call_target="tpu_custom_call" | custom-call | flops 12000000000 | bytes 27262976 | tf_op jit(solution)/shard_map/pallas_call | solution.py:88
  43.4 89.3 %shard_map.85 = (f32[156,1664]{1,0:T(8,128)}, f32[52,1664]{1,0:T(8,128)}, f32[1,1664]{1,0:T(1,128)}, bf16[257,1664]{1,0:T(8,128)(2,1)}) custom-call(bf16[48,104,257]{2,1,0:T(8,128)(2,1)} %bitcast.11, bf16[16,104,257]{2,1,0:T(8,128)(2,1)} %bitcast.10, bf16[257,1664]{1,0:T(8,128)(2,1)} %get-tuple-element.12.lno, bf16[257,1664]{1,0:T(8,128)(2,1)} %get-tuple-element.13.ao, ...), custom_call_target="tpu_custom_call" | custom-call | flops 5692850176 | bytes 16777216 | tf_op jit(solution)/shard_map/pallas_call | solution.py:547
  132.7 0.0 copy-start
  132.7 1.4 reduce
  134.1 2.1 %copy.14 = bf16[1,257,1664]{2,1,0:T(8,128)(2,1)} copy(bf16[1,257,1664]{2,1,0:T(8,128)(2,1)} %bitcast.15) | data formatting | bytes 1710592
  136.2 2.3 %copy.15 = f32[156,1664]{1,0:T(8,128)} copy(f32[156,1664]{1,0:T(8,128)} %get-tuple-element.23) | data formatting | bytes 2076672
  138.5 0.0 copy-done
  138.5 0.7 copy.16
Async XLA Ops:
  132.7 5.8 %copy-start = (f32[52,1664]{1,0:T(8,128)S(1)}, f32[52,1664]{1,0:T(8,128)}, u32[]{:S(2)}) copy-start(f32[52,1664]{1,0:T(8,128)} %get-tuple-element.24) | copy-start | bytes 1038340

commit v3 on v2

--- a/solution.py
+++ b/solution.py
@@ -15,6 +15,8 @@
 
 LANES = 128
 WINDOW = 256
+LOG2_E = 1.4426950408889634
+TOGETHER = 4
 
 
 def dot(a, b, over=((1,), (0,))):
@@ -33,7 +35,7 @@
 
 
 def front_kernel(scale, x_ref, cot_ref, gain_ref, w_ref, wo_ref,
-                 lno_ref, ao_ref, gt_ref, wpad):
+                 lno_ref, ao_ref, gt_ref, ct_ref, wpad):
     h = pl.program_id(0)
     dim = w_ref.shape[2]
 
@@ -43,36 +45,49 @@
         lno_ref[...] = low(normed * gain_ref[...].reshape(1, -1))
         wpad[...] = jnp.zeros_like(wpad)
 
-    for s in range(3):
-        wpad[s * LANES : s * LANES + dim, :] = w_ref[s, 0]
+    pair = range(TOGETHER)
+    for j in pair:
+        for s in range(3):
+            at = (3 * j + s) * LANES
+            wpad[at : at + dim, :] = w_ref[s, j]
     qkv = low(dot(lno_ref[...], wpad[...], ((1,), (1,))))
-    q, k, v = (qkv[:, s * LANES : (s + 1) * LANES] for s in range(3))
-    scores = dot(q, k, ((1,), (1,))) * scale
-    expo = jnp.exp(scores - jnp.max(scores, axis=-1, keepdims=True))
-    prob = expo / jnp.sum(expo, axis=-1, keepdims=True)
-    prob_low = low(prob)
-
-    start = jnp.minimum(lax.div(h * dim, LANES) * LANES, wo_ref.shape[1] - WINDOW)
-    start = pl.multiple_of(start, LANES)
-    offset = h * dim - start
+    q, k, v = ([qkv[:, (3 * j + s) * LANES : (3 * j + s + 1) * LANES] for j in pair] for s in range(3))
+    scores = [dot(q[j], k[j], ((1,), (1,))) for j in pair]
+
     lane = lax.broadcasted_iota(jnp.int32, (1, WINDOW), 1)
-    attn = dot(prob_low, v)
-    attn = jnp.concatenate([attn, jnp.zeros_like(attn)], axis=1)
-    attn = pltpu.roll(attn, offset, 1)
-    window = ao_ref[:, pl.ds(start, WINDOW)].astype(jnp.float32)
-    inside = jnp.logical_and(lane >= offset, lane < offset + dim)
-    ao_ref[:, pl.ds(start, WINDOW)] = low(jnp.where(inside, attn, window))
-
-    grad = dot(cot_ref[...], wo_ref[:, pl.ds(start, WINDOW)])
-    grad = pltpu.roll(grad, lax.rem(WINDOW - offset, WINDOW), 1)[:, :LANES]
-    grad = low(jnp.where(lane[:, :LANES] < dim, grad, 0.0))
-    grad_prob = dot(grad, v, ((1,), (1,)))
-    inner = jnp.sum(grad_prob * prob, axis=-1, keepdims=True)
-    grad_score = low(prob * (grad_prob - inner) * scale)
-
-    gt_ref[0, 0] = low(dot(grad_score, k).T[:dim])
-    gt_ref[1, 0] = low(dot(q, grad_score, ((0,), (0,)))[:dim])
-    gt_ref[2, 0] = low(dot(grad, prob_low, ((0,), (0,)))[:dim])
+    starts = [jnp.minimum(lax.div((h * TOGETHER + j) * dim, LANES) * LANES, wo_ref.shape[1] - WINDOW) for j in pair]
+    starts = [pl.multiple_of(start, LANES) for start in starts]
+    offsets = [(h * TOGETHER + j) * dim - starts[j] for j in pair]
+    grad = [dot(cot_ref[...], wo_ref[:, pl.ds(starts[j], WINDOW)]) for j in pair]
+    back = [lax.rem(WINDOW - offsets[j], WINDOW) for j in pair]
+    grad = [pltpu.roll(grad[j], back[j], 1)[:, :LANES] for j in pair]
+    grad = [low(jnp.where(lane[:, :LANES] < dim, grad[j], 0.0)) for j in pair]
+    grad_prob = [dot(grad[j], v[j], ((1,), (1,))) for j in pair]
+
+    prob = []
+    for j in pair:
+        expo = jnp.exp2((scores[j] - jnp.max(scores[j], axis=-1, keepdims=True)) * (scale * LOG2_E))
+        prob.append(expo * (1.0 / jnp.sum(expo, axis=-1, keepdims=True)))
+    prob_low = [low(prob[j]) for j in pair]
+    attn = [dot(prob_low[j], v[j]) for j in pair]
+    for j in pair:
+        gt_ref[2, j] = low(dot(grad[j], prob_low[j], ((0,), (0,)))[:dim])
+
+    grad_score = []
+    for j in pair:
+        inner = jnp.sum(grad_prob[j] * prob[j], axis=-1, keepdims=True)
+        grad_score.append(low(prob[j] * (grad_prob[j] - inner) * scale))
+    for j in pair:
+        gt_ref[1, j] = low(dot(q[j], grad_score[j], ((0,), (0,)))[:dim])
+        gt_ref[0, j] = low(dot(grad_score[j], k[j]).T[:dim])
+
+    for j in pair:
+        part = cot_ref[:, pl.ds(starts[j], WINDOW)].astype(jnp.float32)
+        ct_ref[j] = low(pltpu.roll(part, back[j], 1)[:, :LANES].T[:dim])
+        wide = pltpu.roll(jnp.concatenate([attn[j], jnp.zeros_like(attn[j])], axis=1), offsets[j], 1)
+        window = ao_ref[:, pl.ds(starts[j], WINDOW)].astype(jnp.float32)
+        inside = jnp.logical_and(lane >= offsets[j], lane < offsets[j] + dim)
+        ao_ref[:, pl.ds(starts[j], WINDOW)] = low(jnp.where(inside, wide, window))
 
 
 def front_call(x, cot, gain, w_qkv, w_out):
@@ -84,14 +99,16 @@
         jax.ShapeDtypeStruct((tok, width), jnp.bfloat16),
         jax.ShapeDtypeStruct((tok, width), jnp.bfloat16),
         jax.ShapeDtypeStruct((3, HEADS, dim, tok), jnp.bfloat16),
+        jax.ShapeDtypeStruct((HEADS, dim, tok), jnp.bfloat16),
     )
     return pl.pallas_call(
         functools.partial(front_kernel, dim**-0.5),
-        grid=(HEADS,),
+        grid=(HEADS // TOGETHER,),
         out_shape=outs,
-        in_specs=[whole(x), whole(cot), whole(gain), pl.BlockSpec((3, 1, dim, width), lambda h: (0, h, 0, 0)), whole(w_out)],
-        out_specs=[whole(outs[0]), whole(outs[1]), pl.BlockSpec((3, 1, dim, tok), lambda h: (0, h, 0, 0))],
-        scratch_shapes=[pltpu.VMEM((3 * LANES, width), jnp.bfloat16)],
+        in_specs=[whole(x), whole(cot), whole(gain), pl.BlockSpec((3, TOGETHER, dim, width), lambda h: (0, h, 0, 0)), whole(w_out)],
+        out_specs=[whole(outs[0]), whole(outs[1]), pl.BlockSpec((3, TOGETHER, dim, tok), lambda h: (0, h, 0, 0)),
+                   pl.BlockSpec((TOGETHER, dim, tok), lambda h: (h, 0, 0))],
+        scratch_shapes=[pltpu.VMEM((TOGETHER * 3 * LANES, width), jnp.bfloat16)],
         compiler_params=pltpu.CompilerParams(vmem_limit_bytes=56 * 2**20, dimension_semantics=("arbitrary",)),
         cost_estimate=pl.CostEstimate(flops=12 * 10**9, bytes_accessed=26 * 2**20, transcendentals=HEADS * tok * tok),
     )(x, cot, gain, w, w_out)
@@ -190,7 +207,7 @@
         if k == 3:
             total = gain_total(k) * factor
             for i in range(cols // LANES):
-                gain_out[:, i * LANES : (i + 1) * LANES] = total[i : i + 1]
+                gain_out[i * LANES : (i + 1) * LANES] = total[i]
 
     def weights(h, slot):
         return pltpu.make_async_copy(w_hbm.at[:, h], wbuf.at[slot], wsem.at[slot])
@@ -549,7 +566,7 @@
         out_shape=(
             jax.ShapeDtypeStruct((Q_ROWS, cols), jnp.float32),
             jax.ShapeDtypeStruct((ROWS - Q_ROWS, cols), jnp.float32),
-            jax.ShapeDtypeStruct((1, cols), jnp.float32),
+            jax.ShapeDtypeStruct((cols,), jnp.float32),
             jax.ShapeDtypeStruct((tok, cols), jnp.bfloat16),
         ),
         in_specs=[vm] * 7 + [pl.BlockSpec(memory_space=pl.ANY)],
@@ -564,12 +581,11 @@
     images = tokens.shape[0] * lax.axis_size("wide") * lax.axis_size("narrow")
     factor = 1.0 / images
     x, cot = tokens[0], cotangent[0]
-    ln_out, attn_out, grad_t = front_call(x, cot, ln_gain, w_qkv, w_out)
-    cot_t = cot.T.reshape(BLOCKS // 2, -1, cot.shape[0])
+    ln_out, attn_out, grad_t, cot_t = front_call(x, cot, ln_gain, w_qkv, w_out)
     grad_t = grad_t.reshape(BLOCKS * 3 // 2, -1, cot.shape[0])
     w = w_qkv.reshape(3, HEADS, -1, cot.shape[1])
     grad_qkv, grad_out, gain, grad_input = reduce_call(grad_t, cot_t, ln_out, attn_out, x, cot, ln_gain, w, factor)
-    return (grad_input[None], grad_qkv, grad_out, gain.reshape(-1))
+    return (grad_input[None], grad_qkv, grad_out, gain)
 
 
 def solution(mesh):

time: 140 us -> 124 us (0.89)
  Pallas kernels: 130 us -> 117 us
  local copies, waits for them, and re-layouts: 7.57 us -> 5.81 us
    pallas_call x1, Pallas kernels: 40.4 us -> 27.8 us  [front_call(): pl.pallas_call(functools.partial(front_kernel, dim ** (-0.5)), grid=(HEAD...]
    reshape x1 -> x0, local copies, waits for them, and re-layouts: 2.42 us -> none  [local(): cot_t = cot.T.reshape(BLOCKS // 2, -1, cot.shape[0])]
    unnamed x5 -> x8, local copies, waits for them, and re-layouts: 5.15 us -> 5.81 us
where the time goes in v3:
time: 124 us
  Pallas kernels  117 us (94%)
  local copies, waits for them, and re-layouts  5.81 us (5%)
    pallas_call x1, Pallas kernels, reduce_call(): pl.pallas_call(functools.partial(reduce_kernel, factor), out_shape=(jax.S...  89.3 us
    pallas_call x1, Pallas kernels, front_call(): pl.pallas_call(functools.partial(front_kernel, dim ** (-0.5)), grid=(HEAD...  27.8 us
    unnamed x8, local copies, waits for them, and re-layouts  5.81 us

profile of v3, /device:TPU:1, one launch (start us, length us, event | category | flops | bytes accessed | tf_op | source)
XLA Modules:
  0.0 123.6 jit_solution(17689831994288913551)
XLA Ops:
  0.6 27.8 %shard_map.84 = (bf16[257,1664]{1,0:T(8,128)(2,1)}, bf16[257,1664]{1,0:T(8,128)(2,1)}, bf16[3,16,104,257]{3,2,1,0:T(8,128)(2,1)}, bf16[16,104,257]{2,1,0:T(8,128)(2,1)}) custom-call(bf16[257,1664]{1,0:T(8,128)(2,1)} %bitcast.9, bf16[257,1664]{1,0:T(8,128)(2,1)} %bitcast.11, f32[1664]{0:T(1024)} %gain_ref.3, bf16[3,16,104,1664]{3,2,1,0:T(8,128)(2,1)} %bitcast.5, ...), custom_call_target="tpu_custom_call" | custom-call | flops 12000000000 | bytes 27262976 | tf_op jit(solution)/shard_map/pallas_call | solution.py:104
  28.4 89.3 %shard_map.85 = (f32[156,1664]{1,0:T(8,128)}, f32[52,1664]{1,0:T(8,128)}, f32[1664]{0:T(1024)}, bf16[257,1664]{1,0:T(8,128)(2,1)}) custom-call(bf16[48,104,257]{2,1,0:T(8,128)(2,1)} %bitcast.7, bf16[16,104,257]{2,1,0:T(8,128)(2,1)} %get-tuple-element.13.ct, bf16[257,1664]{1,0:T(8,128)(2,1)} %get-tuple-element.14.lno, ...), custom_call_target="tpu_custom_call" | custom-call | flops 5692850176 | bytes 16777216 | tf_op jit(solution)/shard_map/pallas_call | solution.py:564
  117.7 0.0 copy-start
  117.8 0.0 copy-start.1
  117.8 2.2 %copy.13 = bf16[1,257,1664]{2,1,0:T(8,128)(2,1)} copy(bf16[1,257,1664]{2,1,0:T(8,128)(2,1)} %bitcast.8) | data formatting | bytes 1710592
  120.0 2.3 %copy.14 = f32[156,1664]{1,0:T(8,128)} copy(f32[156,1664]{1,0:T(8,128)} %get-tuple-element.25) | data formatting | bytes 2076672
  122.2 0.0 copy-done
  122.2 0.7 copy.15
  123.0 0.0 copy-done.1
  123.0 0.6 copy.16
Async XLA Ops:
  117.7 4.5 %copy-start = (f32[52,1664]{1,0:T(8,128)S(1)}, f32[52,1664]{1,0:T(8,128)}, u32[]{:S(2)}) copy-start(f32[52,1664]{1,0:T(8,128)} %get-tuple-element.26) | copy-start | bytes 1038340
  117.8 5.2 %copy-start.1 = (f32[1664]{0:T(1024)S(1)}, f32[1664]{0:T(1024)}, u32[]{:S(2)}) copy-start(f32[1664]{0:T(1024)} %get-tuple-element.27) | copy-start | bytes 19972

commit v4 on v3

--- a/solution.py
+++ b/solution.py
@@ -119,8 +119,8 @@
 Q_ROWS = 156
 PARTS = ((0, 80), (80, 64), (144, 64))
 CUTS = (48, 32, 32)
-RING = 4
-LAG = 2
+RING = 6
+LAG = 4
 MESH = pl.DeviceIdType.MESH
 
 

time: 124 us -> 120 us (0.968)
  Pallas kernels: 117 us -> 113 us
    pallas_call x1, Pallas kernels: 89.3 us -> 85.4 us  [reduce_call(): pl.pallas_call(functools.partial(reduce_kernel, factor), out_shape=(jax.S...]
where the time goes in v4:
time: 120 us
  Pallas kernels  113 us (94%)
  local copies, waits for them, and re-layouts  5.81 us (5%)
    pallas_call x1, Pallas kernels, reduce_call(): pl.pallas_call(functools.partial(reduce_kernel, factor), out_shape=(jax.S...  85.4 us
    pallas_call x1, Pallas kernels, front_call(): pl.pallas_call(functools.partial(front_kernel, dim ** (-0.5)), grid=(HEAD...  27.8 us
    unnamed x8, local copies, waits for them, and re-layouts  5.81 us

profile of v4, /device:TPU:1, one launch (start us, length us, event | category | flops | bytes accessed | tf_op | source)
XLA Modules:
  0.0 119.7 jit_solution(17281210873633197963)
XLA Ops:
  0.6 27.8 %shard_map.84 = (bf16[257,1664]{1,0:T(8,128)(2,1)}, bf16[257,1664]{1,0:T(8,128)(2,1)}, bf16[3,16,104,257]{3,2,1,0:T(8,128)(2,1)}, bf16[16,104,257]{2,1,0:T(8,128)(2,1)}) custom-call(bf16[257,1664]{1,0:T(8,128)(2,1)} %bitcast.9, bf16[257,1664]{1,0:T(8,128)(2,1)} %bitcast.11, f32[1664]{0:T(1024)} %gain_ref.3, bf16[3,16,104,1664]{3,2,1,0:T(8,128)(2,1)} %bitcast.5, ...), custom_call_target="tpu_custom_call" | custom-call | flops 12000000000 | bytes 27262976 | tf_op jit(solution)/shard_map/pallas_call | solution.py:104
  28.4 85.4 %shard_map.85 = (f32[156,1664]{1,0:T(8,128)}, f32[52,1664]{1,0:T(8,128)}, f32[1664]{0:T(1024)}, bf16[257,1664]{1,0:T(8,128)(2,1)}) custom-call(bf16[48,104,257]{2,1,0:T(8,128)(2,1)} %bitcast.7, bf16[16,104,257]{2,1,0:T(8,128)(2,1)} %get-tuple-element.13.ct, bf16[257,1664]{1,0:T(8,128)(2,1)} %get-tuple-element.14.lno, ...), custom_call_target="tpu_custom_call" | custom-call | flops 5692850176 | bytes 16777216 | tf_op jit(solution)/shard_map/pallas_call | solution.py:564
  113.8 0.0 copy-start
  113.8 0.0 copy-start.1
  113.9 2.2 %copy.13 = bf16[1,257,1664]{2,1,0:T(8,128)(2,1)} copy(bf16[1,257,1664]{2,1,0:T(8,128)(2,1)} %bitcast.8) | data formatting | bytes 1710592
  116.0 2.3 %copy.14 = f32[156,1664]{1,0:T(8,128)} copy(f32[156,1664]{1,0:T(8,128)} %get-tuple-element.25) | data formatting | bytes 2076672
  118.3 0.0 copy-done
  118.3 0.7 copy.15
  119.1 0.0 copy-done.1
  119.1 0.6 copy.16
Async XLA Ops:
  113.8 4.5 %copy-start = (f32[52,1664]{1,0:T(8,128)S(1)}, f32[52,1664]{1,0:T(8,128)}, u32[]{:S(2)}) copy-start(f32[52,1664]{1,0:T(8,128)} %get-tuple-element.26) | copy-start | bytes 1038340
  113.8 5.2 %copy-start.1 = (f32[1664]{0:T(1024)S(1)}, f32[1664]{0:T(1024)}, u32[]{:S(2)}) copy-start(f32[1664]{0:T(1024)} %get-tuple-element.27) | copy-start | bytes 19972

commit v5 on v4

--- a/solution.py
+++ b/solution.py
@@ -34,13 +34,15 @@
     return centered * inv_sigma, inv_sigma
 
 
-def front_kernel(scale, x_ref, cot_ref, gain_ref, w_ref, wo_ref,
-                 lno_ref, ao_ref, gt_ref, ct_ref, wpad):
+def front_kernel(scale, x_ref, cot_ref, gain_ref, w_ref, wo_hbm,
+                 lno_ref, ao_ref, gt_ref, ct_ref, wpad, wo_ref, wo_sem):
     h = pl.program_id(0)
     dim = w_ref.shape[2]
+    fetch = pltpu.make_async_copy(wo_hbm, wo_ref, wo_sem)
 
     @pl.when(h == 0)
     def _():
+        fetch.start()
         normed, _ = normalise(x_ref)
         lno_ref[...] = low(normed * gain_ref[...].reshape(1, -1))
         wpad[...] = jnp.zeros_like(wpad)
@@ -58,6 +60,10 @@
     starts = [jnp.minimum(lax.div((h * TOGETHER + j) * dim, LANES) * LANES, wo_ref.shape[1] - WINDOW) for j in pair]
     starts = [pl.multiple_of(start, LANES) for start in starts]
     offsets = [(h * TOGETHER + j) * dim - starts[j] for j in pair]
+    @pl.when(h == 0)
+    def _():
+        fetch.wait()
+
     grad = [dot(cot_ref[...], wo_ref[:, pl.ds(starts[j], WINDOW)]) for j in pair]
     back = [lax.rem(WINDOW - offsets[j], WINDOW) for j in pair]
     grad = [pltpu.roll(grad[j], back[j], 1)[:, :LANES] for j in pair]
@@ -105,10 +111,10 @@
         functools.partial(front_kernel, dim**-0.5),
         grid=(HEADS // TOGETHER,),
         out_shape=outs,
-        in_specs=[whole(x), whole(cot), whole(gain), pl.BlockSpec((3, TOGETHER, dim, width), lambda h: (0, h, 0, 0)), whole(w_out)],
+        in_specs=[whole(x), whole(cot), whole(gain), pl.BlockSpec((3, TOGETHER, dim, width), lambda h: (0, h, 0, 0)), pl.BlockSpec(memory_space=pl.ANY)],
         out_specs=[whole(outs[0]), whole(outs[1]), pl.BlockSpec((3, TOGETHER, dim, tok), lambda h: (0, h, 0, 0)),
                    pl.BlockSpec((TOGETHER, dim, tok), lambda h: (h, 0, 0))],
-        scratch_shapes=[pltpu.VMEM((TOGETHER * 3 * LANES, width), jnp.bfloat16)],
+        scratch_shapes=[pltpu.VMEM((TOGETHER * 3 * LANES, width), jnp.bfloat16), pltpu.VMEM(w_out.shape, jnp.bfloat16), pltpu.SemaphoreType.DMA],
         compiler_params=pltpu.CompilerParams(vmem_limit_bytes=56 * 2**20, dimension_semantics=("arbitrary",)),
         cost_estimate=pl.CostEstimate(flops=12 * 10**9, bytes_accessed=26 * 2**20, transcendentals=HEADS * tok * tok),
     )(x, cot, gain, w, w_out)

time: 120 us -> 120 us (level)
  no operation moved by 1% of the time
where the time goes in v5:
time: 120 us; the launch traced here: 119 us
  Pallas kernels  112 us (93%)
  local copies, waits for them, and re-layouts  5.81 us (5%)
    pallas_call x1, Pallas kernels, reduce_call(): pl.pallas_call(functools.partial(reduce_kernel, factor), out_shape=(jax.S...  85.4 us
    pallas_call x1, Pallas kernels, front_call(): pl.pallas_call(functools.partial(front_kernel, dim ** (-0.5)), grid=(HEAD...  26.9 us
    unnamed x8, local copies, waits for them, and re-layouts  5.81 us

profile of v5, /device:TPU:1, one launch (start us, length us, event | category | flops | bytes accessed | tf_op | source)
XLA Modules:
  0.0 118.8 jit_solution(17923646591271082986)
XLA Ops:
  0.6 26.9 %shard_map.84 = (bf16[257,1664]{1,0:T(8,128)(2,1)}, bf16[257,1664]{1,0:T(8,128)(2,1)}, bf16[3,16,104,257]{3,2,1,0:T(8,128)(2,1)}, bf16[16,104,257]{2,1,0:T(8,128)(2,1)}) custom-call(bf16[257,1664]{1,0:T(8,128)(2,1)} %bitcast.9, bf16[257,1664]{1,0:T(8,128)(2,1)} %bitcast.11, f32[1664]{0:T(1024)} %gain_ref.3, bf16[3,16,104,1664]{3,2,1,0:T(8,128)(2,1)} %bitcast.5, ...), custom_call_target="tpu_custom_call" | custom-call | flops 12000000000 | bytes 27262976 | tf_op jit(solution)/shard_map/pallas_call | solution.py:110
  27.6 85.4 %shard_map.85 = (f32[156,1664]{1,0:T(8,128)}, f32[52,1664]{1,0:T(8,128)}, f32[1664]{0:T(1024)}, bf16[257,1664]{1,0:T(8,128)(2,1)}) custom-call(bf16[48,104,257]{2,1,0:T(8,128)(2,1)} %bitcast.7, bf16[16,104,257]{2,1,0:T(8,128)(2,1)} %get-tuple-element.13.ct, bf16[257,1664]{1,0:T(8,128)(2,1)} %get-tuple-element.14.lno, ...), custom_call_target="tpu_custom_call" | custom-call | flops 5692850176 | bytes 16777216 | tf_op jit(solution)/shard_map/pallas_call | solution.py:570
  113.0 0.0 copy-start
  113.0 0.0 copy-start.1
  113.0 2.2 %copy.13 = bf16[1,257,1664]{2,1,0:T(8,128)(2,1)} copy(bf16[1,257,1664]{2,1,0:T(8,128)(2,1)} %bitcast.8) | data formatting | bytes 1710592
  115.2 2.3 %copy.14 = f32[156,1664]{1,0:T(8,128)} copy(f32[156,1664]{1,0:T(8,128)} %get-tuple-element.25) | data formatting | bytes 2076672
  117.5 0.0 copy-done
  117.5 0.7 copy.15
  118.2 0.0 copy-done.1
  118.2 0.6 copy.16
Async XLA Ops:
  113.0 4.5 %copy-start = (f32[52,1664]{1,0:T(8,128)S(1)}, f32[52,1664]{1,0:T(8,128)}, u32[]{:S(2)}) copy-start(f32[52,1664]{1,0:T(8,128)} %get-tuple-element.26) | copy-start | bytes 1038340
  113.0 5.2 %copy-start.1 = (f32[1664]{0:T(1024)S(1)}, f32[1664]{0:T(1024)}, u32[]{:S(2)}) copy-start(f32[1664]{0:T(1024)} %get-tuple-element.27) | copy-start | bytes 19972

commit v6 on v5

--- a/solution.py
+++ b/solution.py
@@ -223,20 +223,21 @@
         gln[...] = jnp.zeros_like(gln)
         wpad[...] = jnp.zeros_like(wpad)
 
-        @pl.loop(0, HEADS)
-        def _(h):
-            slot = rem(h, 2)
-            weights(h, slot).wait()
-
-            @pl.when(h < HEADS - 1)
-            def _():
-                weights(h + 1, 1 - slot).start()
-
+        @pl.loop(0, HEADS // 2)
+        def _(n):
             pad = jnp.zeros((LANES - dim, gt.shape[2]), jnp.float32)
             stack = []
-            for s in range(3):
-                wpad[s * LANES : s * LANES + dim, :] = wbuf[slot, s]
-                stack += [gt[s * HEADS + h].astype(jnp.float32), pad]
+            for slot in range(2):
+                weights(2 * n + slot, slot).wait()
+                for s in range(3):
+                    at = (3 * slot + s) * LANES
+                    wpad[at : at + dim, :] = wbuf[slot, s]
+                    stack += [gt[s * HEADS + 2 * n + slot].astype(jnp.float32), pad]
+
+                @pl.when(n < HEADS // 2 - 1)
+                def _():
+                    weights(2 * n + 2 + slot, slot).start()
+
             gln[...] += dot(low(jnp.concatenate(stack, axis=0).T), wpad[...])
 
         normed, inv_sigma = normalise(x_ref)
@@ -263,6 +264,9 @@
         for k in range(full, right.shape[0]):
             total = total + left[:, k : k + 1] * right[k : k + 1, lo:hi].astype(jnp.float32)
         return total * factor
+
+    def block_at(side, b):
+        return side["S"].at[div(b, 8), rem(div(b, 4), 2), rem(div(b, 2), 2), rem(b, 2)]
 
     def fill(side, span, b, slot):
         even, odd = rows_of_pair(b)
@@ -276,11 +280,11 @@
             hi = min(width, lo + 512)
             p = product(first, lno, span[0] + lo, span[0] + hi)
             q = product(last, ao, span[0] + lo, span[0] + hi)
-            for k, dst, at in ((0, side["T0"], slot), (1, side["S"], b)):
+            for k, dst in ((0, side["T0"].at[slot]), (1, block_at(side, b))):
                 u, v = p[160 * k : 160 * k + 160], q[64 * k : 64 * k + 64]
-                dst[at, 0:144, lo:hi] = low(u[0:144])
-                dst[at, 144:160, lo:hi] = low(jnp.where(line < Q_ROWS - 144, u[144:160], v[0:16]))
-                dst[at, 160:208, lo:hi] = low(v[16:64])
+                dst[0:144, lo:hi] = low(u[0:144])
+                dst[144:160, lo:hi] = low(jnp.where(line < Q_ROWS - 144, u[144:160], v[0:16]))
+                dst[160:208, lo:hi] = low(v[16:64])
 
     def core_copy(side, b, slot):
         return remote(side["T0"].at[slot], side["R0"].at[b], side["sems"][0].at[b], side["sems"][1].at[b], mate)
@@ -305,7 +309,7 @@
             def _():
                 b = n - LAG
                 core_copy(side, b, 0).wait_recv()
-                accumulate(side["S"].at[b], side["R0"].at[b])
+                accumulate(block_at(side, b), side["R0"].at[b])
 
         for n in range(16 - RING, 16):
             core_copy(side, n, n % RING).wait_send()
@@ -323,47 +327,51 @@
     )
 
     def part(h, p, b):
-        return sides[h]["S"].at[b, pl.ds(*PARTS[p]), :]
-
-    def half_copy(h, p, to, i, src):
+        return block_at(sides[h], b).at[pl.ds(*PARTS[p]), :]
+
+    def two(h, p, t, g):
+        rows = pl.ds(*PARTS[p])
+        t_hi, t_lo = div(t, 2), rem(t, 2)
+        if p == 0:
+            return sides[h]["S"].at[g, t_hi, t_lo, :, rows, :]
+        if p == 1:
+            return sides[h]["S"].at[g, :, rem(c + t + g, 2), t_hi, rows, :]
+        return sides[h]["S"].at[t_hi, g, :, t_lo, rows, :]
+
+    def half_copy(h, p, to, src):
         sems = sides[h]["sems"]
-        return remote(src, sides[h]["halves"][p].at[to, i], sems[2].at[p, to, i], sems[3].at[p, to, i],
+        return remote(src, sides[h]["halves"][p].at[to], sems[2].at[p, to], sems[3].at[p, to],
                       shift(orders[p][0], 1 + 2 * to))
 
-    def whole_copy(h, p, to, i, src):
+    def whole_copy(h, p, to, g, src):
         sems = sides[h]["sems"]
-        return remote(src, sides[h]["wholes"][p].at[to, i], sems[4].at[p, to, i], sems[5].at[p, to, i],
+        return remote(src, sides[h]["wholes"][p].at[to, pl.ds(2 * g, 2)], sems[4].at[p, to, g], sems[5].at[p, to, g],
                       shift(orders[p][0], 1 + 2 * to))
 
+    def any_whole(h, p, to, g):
+        return whole_copy(h, p, to, g, sides[h]["wholes"][p].at[to, pl.ds(2 * g, 2)])
+
     six = [(p, to) for to in range(2) for p in range(3)]
 
     def first_sends(h):
-        for i in range(2):
-            for p, to in six:
-                t = rem(place[orders[p][0]] + 2, 4)
-                half_copy(h, p, to, i, part(h, p, firsts[p](t, i + 2 * to))).start()
-        for i in range(2):
-            for p, to in six:
-                t = rem(place[orders[p][0]] + 1 + 2 * to, 4)
-                index = i + 2 - 2 * to
-                whole_copy(h, p, to, index, part(h, p, firsts[p](t, index))).start()
+        for p, to in six:
+            half_copy(h, p, to, two(h, p, rem(place[orders[p][0]] + 2, 4), to)).start()
+        for p, to in six:
+            t = rem(place[orders[p][0]] + 1 + 2 * to, 4)
+            whole_copy(h, p, to, 1 - to, two(h, p, t, 1 - to)).start()
 
     def first_relays(h):
-        for i in range(2):
-            for p, to in six:
-                halves = sides[h]["halves"][p]
-                half_copy(h, p, to, i, halves.at[to, i]).wait_recv()
-                t = rem(place[orders[p][0]] + 1 + 2 * to, 4)
-                index = i + 2 * to
-                block = part(h, p, firsts[p](t, index))
-                accumulate(block, halves.at[to, i])
-                whole_copy(h, p, to, index, block).start()
+        for p, to in six:
+            halves = sides[h]["halves"][p]
+            half_copy(h, p, to, halves.at[to]).wait_recv()
+            t = rem(place[orders[p][0]] + 1 + 2 * to, 4)
+            for i in range(2):
+                accumulate(part(h, p, firsts[p](t, i + 2 * to)), halves.at[to, i])
+            whole_copy(h, p, to, to, two(h, p, t, to)).start()
 
     def ready(h, p, t):
         b, i = seconds[p](t)
         wholes = sides[h]["wholes"][p]
-        for to in range(2):
-            whole_copy(h, p, to, i, wholes.at[to, i]).wait_recv()
         accumulate(part(h, p, b), wholes.at[0, i], wholes.at[1, i])
         return part(h, p, b)
 
@@ -380,6 +388,9 @@
 
     def second_sends(h):
         for p in range(3):
+            for to in range(2):
+                for g in range(2):
+                    any_whole(h, p, to, g).wait_recv()
             opposite = ready(h, p, rem(place[orders[p][1]] + 2, 4))
             second_copy(h, p, 0, opposite).start()
             second_copy(h, p, 1, opposite).start()
@@ -492,10 +503,9 @@
     def drain(h):
         for p in range(3):
             for to in range(2):
-                for i in range(4):
-                    whole_copy(h, p, to, i, sides[h]["wholes"][p].at[to, i]).wait_send()
-                for i in range(2):
-                    half_copy(h, p, to, i, sides[h]["halves"][p].at[to, i]).wait_send()
+                for g in range(2):
+                    any_whole(h, p, to, g).wait_send()
+                half_copy(h, p, to, sides[h]["halves"][p].at[to]).wait_send()
             for k in range(6):
                 second_copy(h, p, k, mine(h, p)).wait_send()
 
@@ -519,6 +529,7 @@
                     third(h, mine(h, p), sides[h]["C"][p].at[r], base + r, where()).wait_send()
 
     weights(0, 0).start()
+    weights(1, 1).start()
     produce(0)
     first_sends(0)
     produce(1)
@@ -557,16 +568,16 @@
     dim = gt.shape[1]
     scratch = [
         pltpu.VMEM((4, 4, 16, LANES), jnp.float32), dma((4, 3)), dma((4, 3)),
-        pltpu.VMEM((2, 3, dim, cols), jnp.bfloat16), pltpu.VMEM((3 * LANES, cols), jnp.bfloat16),
+        pltpu.VMEM((2, 3, dim, cols), jnp.bfloat16), pltpu.VMEM((6 * LANES, cols), jnp.bfloat16),
         pltpu.VMEM((tok, cols), jnp.float32), pltpu.VMEM((1, cols), jnp.float32), dma((2,)),
     ]
     for lo, hi in column_halves(cols):
         bf = lambda *shape: pltpu.VMEM(shape + (hi - lo,), jnp.bfloat16)
         sizes = [size for _, size in PARTS]
-        scratch += [bf(16, ROWS), bf(16, ROWS), bf(RING, ROWS)]
+        scratch += [bf(2, 2, 2, 2, ROWS), bf(16, ROWS), bf(RING, ROWS)]
         scratch += [x for s in sizes for x in (bf(2, 2, s), bf(2, 4, s), bf(3, s))]
         scratch += [bf(2, sizes[0]), bf(3, sizes[1]), bf(3, sizes[2]), bf(sizes[0]), bf(ROWS)]
-        scratch += [dma((16,))] * 2 + [dma((3, 2, 2))] * 2 + [dma((3, 2, 4))] * 2 + [dma((3, 6))] * 2 + [dma((11,))] * 2
+        scratch += [dma((16,))] * 2 + [dma((3, 2))] * 2 + [dma((3, 2, 2))] * 2 + [dma((3, 6))] * 2 + [dma((11,))] * 2
     return pl.pallas_call(
         functools.partial(reduce_kernel, factor),
         out_shape=(

time: 120 us -> 117 us (0.975)
  Pallas kernels: 112 us -> 110 us
    pallas_call x1, Pallas kernels: 85.4 us -> 83.2 us  [reduce_call(): pl.pallas_call(functools.partial(reduce_kernel, factor), out_shape=(jax.S...]
where the time goes in v6:
time: 117 us
  Pallas kernels  110 us (94%)
  local copies, waits for them, and re-layouts  5.81 us (5%)
    pallas_call x1, Pallas kernels, reduce_call(): pl.pallas_call(functools.partial(reduce_kernel, factor), out_shape=(jax.S...  83.2 us
    pallas_call x1, Pallas kernels, front_call(): pl.pallas_call(functools.partial(front_kernel, dim ** (-0.5)), grid=(HEAD...  26.9 us
    unnamed x8, local copies, waits for them, and re-layouts  5.81 us

profile of v6, /device:TPU:1, one launch (start us, length us, event | category | flops | bytes accessed | tf_op | source)
XLA Modules:
  0.0 116.6 jit_solution(15684609478191257930)
XLA Ops:
  0.6 26.9 %shard_map.84 = (bf16[257,1664]{1,0:T(8,128)(2,1)}, bf16[257,1664]{1,0:T(8,128)(2,1)}, bf16[3,16,104,257]{3,2,1,0:T(8,128)(2,1)}, bf16[16,104,257]{2,1,0:T(8,128)(2,1)}) custom-call(bf16[257,1664]{1,0:T(8,128)(2,1)} %bitcast.9, bf16[257,1664]{1,0:T(8,128)(2,1)} %bitcast.11, f32[1664]{0:T(1024)} %gain_ref.3, bf16[3,16,104,1664]{3,2,1,0:T(8,128)(2,1)} %bitcast.5, ...), custom_call_target="tpu_custom_call" | custom-call | flops 12000000000 | bytes 27262976 | tf_op jit(solution)/shard_map/pallas_call | solution.py:110
  27.6 83.2 %shard_map.85 = (f32[156,1664]{1,0:T(8,128)}, f32[52,1664]{1,0:T(8,128)}, f32[1664]{0:T(1024)}, bf16[257,1664]{1,0:T(8,128)(2,1)}) custom-call(bf16[48,104,257]{2,1,0:T(8,128)(2,1)} %bitcast.7, bf16[16,104,257]{2,1,0:T(8,128)(2,1)} %get-tuple-element.13.ct, bf16[257,1664]{1,0:T(8,128)(2,1)} %get-tuple-element.14.lno, ...), custom_call_target="tpu_custom_call" | custom-call | flops 5692850176 | bytes 16777216 | tf_op jit(solution)/shard_map/pallas_call | solution.py:581
  110.8 0.0 copy-start
  110.8 0.0 copy-start.1
  110.8 2.2 %copy.13 = bf16[1,257,1664]{2,1,0:T(8,128)(2,1)} copy(bf16[1,257,1664]{2,1,0:T(8,128)(2,1)} %bitcast.8) | data formatting | bytes 1710592
  113.0 2.3 %copy.14 = f32[156,1664]{1,0:T(8,128)} copy(f32[156,1664]{1,0:T(8,128)} %get-tuple-element.25) | data formatting | bytes 2076672
  115.3 0.0 copy-done
  115.3 0.7 copy.15
  116.0 0.0 copy-done.1
  116.0 0.6 copy.16
Async XLA Ops:
  110.8 4.5 %copy-start = (f32[52,1664]{1,0:T(8,128)S(1)}, f32[52,1664]{1,0:T(8,128)}, u32[]{:S(2)}) copy-start(f32[52,1664]{1,0:T(8,128)} %get-tuple-element.26) | copy-start | bytes 1038340
  110.8 5.2 %copy-start.1 = (f32[1664]{0:T(1024)S(1)}, f32[1664]{0:T(1024)}, u32[]{:S(2)}) copy-start(f32[1664]{0:T(1024)} %get-tuple-element.27) | copy-start | bytes 19972
